TPU v7x, 256 devices: a whole 4x4x8 slice. The times are simulated.
256 devices in a mesh: row: 8 (over y, z_hi), col: 32 (over z_lo, x, core).
Axes of the slice: x: 4, y: 4, z: 8 (z_hi: 2, z_lo: 4; z = z_hi * 4 + z_lo), core: 2. Of those that a mesh axis runs over, the one named last changes fastest.
Arguments:
- features: bfloat16 [262144, 128], P(('col', 'row')), may hold values from -6 to 6
- weight: bfloat16 [128, 128], replicated, may hold values from -0.5 to 0.5
- tile_values: bfloat16 [8, 32, 64, 128, 128], P('row', 'col'), may hold values from -0.25 to 0.25
- tile_rows: int32 [8, 32, 64], P('row', 'col'), may hold values from 0 to 255, as said below
- tile_cols: int32 [8, 32, 64], P('row', 'col'), may hold values from 0 to 63
- tile_live: int32 [8, 32], P('row', 'col'), may hold values from 8 to 64, as said below
- cotangent: bfloat16 [262144, 128], P(('row', 'col')), may hold values from -6 to 6
Outputs:
- layer_out: bfloat16 [262144, 128], P(('row', 'col'))
- grad_x: bfloat16 [262144, 128], P(('col', 'row'))
- grad_w: float32 [128, 128], replicated
Inputs may be any that keep to these rules, and one draw needn't show every extreme that they name: `tile_live`: slots at or beyond a device's count are ignored; some device has all 64 slots live, and each count is 64 divided by 1, 2, 4 or 8. `tile_rows`: over all 64 slots of one device, at most 4 name block rows c * 8 to c * 8 + 7 for any one c; in every grid row some c receives exactly 4 such slots from every device of that row, and these are the devices' first slots.
All inputs are finite; a program needn't handle non-finite values.
Results may differ from a plain program's by a relative error of at most 0.022.
Values may be sent and summed in bfloat16 or wider, within the bound.
A program may use at most 64 MiB of HBM per device.

v0:
```python
import jax
import jax.numpy as jnp
from jax import lax
from jax.sharding import PartitionSpec as P


def silu_slope(value):
    sigma = jax.nn.sigmoid(value)
    return sigma * (1.0 + value * (1.0 - sigma))


def turn_count(tiles, per_turn):
    return tiles // per_turn


def aggregate_forward(entries, col_list, live_count, source, out_blocks, target_index):
    tiles = entries.shape[0]
    per_turn = min(32, tiles)
    width = source.shape[2]
    edge = entries.shape[1]

    def advance(turn_index, accumulated):
        start = turn_index * per_turn
        piece = lax.dynamic_slice_in_dim(entries, start, per_turn, 0)
        target_piece = lax.dynamic_slice_in_dim(target_index, start, per_turn, 0)
        col_piece = lax.dynamic_slice_in_dim(col_list, start, per_turn, 0)
        keep_tile = start + jnp.arange(per_turn, dtype=jnp.int32) < live_count
        product = jnp.einsum(
            "tij,tjf->tif", piece, source[col_piece], preferred_element_type=jnp.float32
        )
        product = jnp.where(keep_tile[:, None, None], product, 0.0)
        return accumulated.at[target_piece].add(product)

    initial = jnp.zeros((out_blocks, edge, width), jnp.float32)
    return lax.fori_loop(0, turn_count(tiles, per_turn), advance, initial)


def aggregate_backward(entries, row_list, col_list, live_count, source, out_blocks):
    tiles = entries.shape[0]
    per_turn = min(32, tiles)
    width = source.shape[2]
    edge = entries.shape[1]

    def advance(turn_index, accumulated):
        start = turn_index * per_turn
        piece = lax.dynamic_slice_in_dim(entries, start, per_turn, 0)
        row_piece = lax.dynamic_slice_in_dim(row_list, start, per_turn, 0)
        col_piece = lax.dynamic_slice_in_dim(col_list, start, per_turn, 0)
        keep_tile = start + jnp.arange(per_turn, dtype=jnp.int32) < live_count
        product = jnp.einsum(
            "tij,tif->tjf", piece, source[row_piece], preferred_element_type=jnp.float32
        )
        product = jnp.where(keep_tile[:, None, None], product, 0.0)
        return accumulated.at[col_piece].add(product)

    initial = jnp.zeros((out_blocks, edge, width), jnp.float32)
    return lax.fori_loop(0, turn_count(tiles, per_turn), advance, initial)


def shards(features, weight, tile_values, tile_rows, tile_cols, tile_live, cotangent):
    tile_edge = tile_values.shape[-1]
    width = weight.shape[1]
    entries = tile_values[0, 0]
    row_list = tile_rows[0, 0]
    col_list = tile_cols[0, 0]
    live_count = tile_live[0, 0]
    own_blocks = features.shape[0] // tile_edge
    groups = lax.axis_size("col")
    own_proj = jnp.dot(features, weight, preferred_element_type=jnp.float32).astype(jnp.bfloat16)
    projected = lax.all_gather(own_proj, "row", axis=0, tiled=True)
    source = projected.reshape(-1, tile_edge, width)
    row_blocks = own_blocks * groups
    partial_value = aggregate_forward(entries, col_list, live_count, source, row_blocks, row_list)
    preact = lax.psum_scatter(
        partial_value.reshape(-1, width).astype(jnp.bfloat16),
        "col",
        scatter_dimension=0,
        tiled=True,
    ).astype(jnp.float32)
    layer_out = jax.nn.silu(preact).astype(jnp.bfloat16)
    grad_pre = (cotangent.astype(jnp.float32) * silu_slope(preact)).astype(jnp.bfloat16)
    grad_rows = lax.all_gather(grad_pre, "col", axis=0, tiled=True).reshape(-1, tile_edge, width)
    partial_back = aggregate_backward(
        entries, row_list, col_list, live_count, grad_rows, source.shape[0]
    )
    partial_back = partial_back.reshape(-1, width)
    grad_proj = lax.psum_scatter(
        partial_back.astype(jnp.bfloat16), "row", scatter_dimension=0, tiled=True
    ).astype(jnp.float32)
    weight_term = jnp.dot(
        features.astype(jnp.float32).T, grad_proj, precision=lax.Precision.HIGHEST
    )
    grad_w = lax.psum(weight_term, ("row", "col"))
    grad_x = jnp.dot(
        grad_proj, weight.astype(jnp.float32).T, precision=lax.Precision.HIGHEST
    ).astype(jnp.bfloat16)
    return (layer_out, grad_x, grad_w)


def solution(mesh):
    in_specs = (
        P(("col", "row"), None),
        P(),
        P("row", "col", None, None, None),
        P("row", "col", None),
        P("row", "col", None),
        P("row", "col"),
        P(("row", "col"), None),
    )
    out_specs = (P(("row", "col"), None), P(("col", "row"), None), P())
    return jax.shard_map(shards, mesh=mesh, in_specs=in_specs, out_specs=out_specs, check_vma=False)
```

profile of v0, /device:TPU:1, one launch (start us, length us, event | category | flops | bytes accessed | tf_op | source)
XLA Modules:
  0.0 726.1 jit_solution(623631342405290673)
XLA Ops:
  7.2 0.0 all-gather.3.cloned.1.call-start
  7.2 0.9 copy-done
  8.1 1.7 convolution_convert_fusion.1
  9.8 0.0 all-gather.3.cloned.1.call-update
  9.8 0.0 reduce-scatter.3.cloned.1.call-start
  9.9 80.1 %all-gather.3.cloned.1.call-done = bf16[8192,128]{1,0:T(8,128)(2,1)} async-done(((bf16[1024,128]{1,0:T(8,128)(2,1)}), bf16[8192,128]{1,0:T(8,128)(2,1)}) %all-gather.3.cloned.1.call-update) | async-done | bytes 2097168 | tf_op jit(solution)/shard_map/all_gather | solution.py:70
  90.0 7.9 %broadcast_in_dim.88 = f32[256,128,128]{2,1,0:T(8,128)} broadcast(f32[]{:T(128)} %constant.91.clone.1), dimensions={} | broadcast | bytes 16777220 | tf_op jit(solution)/shard_map/broadcast_in_dim | solution.py:34
  97.9 22.0 %while.26 = (s32[]{:T(128)}, f32[256,128,128]{2,1,0:T(8,128)}, s32[64]{0:T(128)S(1)}, s32[]{:T(128)}, bf16[64,128,128]{2,1,0:T(8,128)(2,1)}, /*index=5*/s32[64]{...) while((s32[]{:T(128)}, f32[256,128,128]{2,1,0:T(8,128)}, ...), condition=%wide.region_2.3_spmd, body=%wide.region_0.2_spmd.sunk | while | flops 135267584 | bytes 12588139 | solution.py:35
  97.9 0.1 compare_select_fusion.6
  97.9 2.3 gather_fusion
  100.3 0.7 add_compare_fusion.4
  101.0 1.7 convolution_select_fusion.4
  102.6 6.3 scatter_fusion
  108.9 0.1 compare_select_fusion.6
  109.0 2.3 gather_fusion
  111.3 0.7 add_compare_fusion.4
  112.0 1.7 convolution_select_fusion.4
  113.6 6.2 scatter_fusion
  119.9 9.2 %convert_element_type.34 = bf16[256,128,128]{2,1,0:T(8,128)(2,1)} convert(f32[256,128,128]{2,1,0:T(8,128)} %get-tuple-element.251) | non-fusion elementwise | flops 4194304 | bytes 25165824 | tf_op jit(solution)/shard_map/convert_element_type | solution.py:75
  129.1 0.0 reduce-scatter.3.cloned.1.call-update
  129.1 0.0 all-gather.5.cloned.1.call-start
  129.1 149.0 %reduce-scatter.3.cloned.1.call-done = bf16[1024,128]{1,0:T(8,128)(2,1)} async-done(((bf16[32768,128]{1,0:T(8,128)(2,1)}), bf16[1024,128]{1,0:T(8,128)(2,1)}) %reduce-scatter.3.cloned.1.call-update) | async-done | bytes 262160 | tf_op jit(solution)/shard_map/reduce_scatter | solution.py:74
  278.2 2.0 fusion.11
  280.2 0.0 all-gather.5.cloned.1.call-update
  280.2 0.0 reduce-scatter.5.cloned.1.call-start
  280.2 3.0 copy.10
  283.2 68.7 %all-gather.5.cloned.1.call-done = bf16[32768,128]{1,0:T(8,128)(2,1)} async-done(((bf16[1024,128]{1,0:T(8,128)(2,1)}), bf16[32768,128]{1,0:T(8,128)(2,1)}) %all-gather.5.cloned.1.call-update) | async-done | bytes 8388624 | tf_op jit(solution)/shard_map/all_gather | solution.py:82
  351.9 2.5 broadcast_in_dim.89
  354.4 25.3 %while.27 = (s32[]{:T(128)}, f32[64,128,128]{2,1,0:T(8,128)}, s32[64]{0:T(128)S(1)}, s32[]{:T(128)}, bf16[64,128,128]{1,2,0:T(8,128)(2,1)}, /*index=5*/s32[64]{0...) while((s32[]{:T(128)}, f32[64,128,128]{2,1,0:T(8,128)}, ...), condition=%wide.region_6.7_spmd, body=%wide.region_4.6_spmd.sunk | while | flops 135267584 | bytes 12588139 | solution.py:57
  354.4 0.1 compare_select_fusion.7
  354.5 4.1 gather_fusion.1
  358.6 0.7 add_compare_fusion.5
  359.3 1.7 convolution_select_fusion.5
  360.9 6.1 scatter_fusion.1
  367.1 0.1 compare_select_fusion.7
  367.1 4.1 gather_fusion.1
  371.3 0.7 add_compare_fusion.5
  371.9 1.7 convolution_select_fusion.5
  373.6 6.1 scatter_fusion.1
  379.7 3.9 convert_element_type.40
  383.6 0.0 reduce-scatter.5.cloned.1.call-update
  383.6 0.0 all-reduce.2.cloned.1.call-start
  383.7 92.3 %reduce-scatter.5.cloned.1.call-done = bf16[1024,128]{1,0:T(8,128)(2,1)} async-done(((bf16[8192,128]{1,0:T(8,128)(2,1)}), bf16[1024,128]{1,0:T(8,128)(2,1)}) %reduce-scatter.5.cloned.1.call-update) | async-done | bytes 262160 | tf_op jit(solution)/shard_map/reduce_scatter | solution.py:87
  476.0 1.8 convolution_bitcast_fusion
  477.9 0.0 all-reduce.2.cloned.1.call-update
  477.9 1.9 convolution_convert_fusion
  479.8 238.2 %all-reduce.2.cloned.1.call-done = f32[128,128]{0,1:T(8,128)} async-done(((f32[128,128]{0,1:T(8,128)}), f32[128,128]{0,1:T(8,128)}) %all-reduce.2.cloned.1.call-update) | async-done | bytes 65552 | tf_op jit(solution)/shard_map/psum | solution.py:93
  718.0 1.6 copy.12
  (15 shorter events, 0.1 us)
Async XLA Ops:
  7.2 1.0 copy-start
  7.2 82.8 %all-gather.3.cloned.1.call-start = ((), (), s32[]{:S(2)}) async-start(), calls=%async_computation.2 | async-start | bytes 2359296 | tf_op jit(solution)/shard_map/all_gather | solution.py:70
  9.8 268.3 %reduce-scatter.3.cloned.1.call-start = ((), (), s32[]{:S(2)}) async-start(), calls=%async_computation.3 | async-start | bytes 8650752 | tf_op jit(solution)/shard_map/reduce_scatter | solution.py:74
  90.0 7.9 %copy-start.4 = (s32[1,1,64]{2,1,0:T(1,128)S(1)}, s32[1,1,64]{2,1,0:T(1,128)}, u32[]{:S(2)}) copy-start(s32[1,1,64]{2,1,0:T(1,128)} %param.14) | copy-start | bytes 772
  90.0 7.9 %copy-start.5 = (s32[1,1,64]{2,1,0:T(1,128)S(1)}, s32[1,1,64]{2,1,0:T(1,128)}, u32[]{:S(2)}) copy-start(s32[1,1,64]{2,1,0:T(1,128)} %param.15) | copy-start | bytes 772
  129.1 149.1 %copy-start.2 = (bf16[1024,128]{1,0:T(8,128)(2,1)S(1)}, bf16[1024,128]{1,0:T(8,128)(2,1)}, u32[]{:S(2)}) copy-start(bf16[1024,128]{1,0:T(8,128)(2,1)} %param.17) | copy-start | bytes 786436
  129.1 151.2 %copy-start.1 = (bf16[64,128,128]{2,1,0:T(8,128)(2,1)S(1)}, bf16[64,128,128]{2,1,0:T(8,128)(2,1)}, u32[]{:S(2)}) copy-start(bf16[64,128,128]{2,1,0:T(8,128)(2,1)} %get-tuple-element.464) | copy-start | bytes 6291460
  129.1 222.8 %all-gather.5.cloned.1.call-start = ((), (), s32[]{:S(2)}) async-start(), calls=%async_computation.4 | async-start | bytes 8650752 | tf_op jit(solution)/shard_map/all_gather | solution.py:82
  280.2 195.8 %reduce-scatter.5.cloned.1.call-start = ((), (), s32[]{:S(2)}) async-start(), calls=%async_computation.5 | async-start | bytes 2359296 | tf_op jit(solution)/shard_map/reduce_scatter | solution.py:87
  383.6 94.3 %copy-start.3 = (bf16[128,128]{1,0:T(8,128)(2,1)S(1)}, bf16[128,128]{1,0:T(8,128)(2,1)}, u32[]{:S(2)}) copy-start(bf16[128,128]{1,0:T(8,128)(2,1)} %param.12) | copy-start | bytes 98308
  383.6 334.3 %all-reduce.2.cloned.1.call-start = ((), (), s32[]{:S(2)}) async-start(), calls=%async_computation.6 | async-start | bytes 131072 | tf_op jit(solution)/shard_map/psum | solution.py:93
Sparse Core Ops, SparseCore 0:
  11.2 78.7 all-gather.2
  129.2 148.9 reduce-scatter.2
  280.6 71.2 all-gather.4
  383.8 92.2 reduce-scatter.4
  482.8 235.0 all-reduce.1
where the time goes:
time: 727 us; the launch traced here: 726 us
  waiting for transfers between devices  628 us (86%)
  other arithmetic  42.8 us (6%)
  local copies, waits for them, and re-layouts  28.7 us (4%)
  between operations  13.8 us (2%)
  matrix products  12 us (2%)
    psum x1, waiting for transfers between devices, shards(): grad_w = lax.psum(weight_term, ('row', 'col'))  238 us
    reduce_scatter x1, waiting for transfers between devices, shards(): lax.psum_scatter(partial_value.reshape(-1, width).astype(jnp.bfloat16), '...  149 us
    reduce_scatter x1, waiting for transfers between devices, shards(): lax.psum_scatter(partial_back.astype(jnp.bfloat16), 'row', scatter_dimens...  92.3 us
    all_gather x1, waiting for transfers between devices, shards(): projected = lax.all_gather(own_proj, 'row', axis=0, tiled=True)  80.1 us
    all_gather x1, waiting for transfers between devices, shards(): lax.all_gather(grad_pre, 'col', axis=0, tiled=True)  68.7 us
  transfers between devices with their start and end apart: 5, of which 5 were waited for; matrix products, arithmetic and copies ran while one was open for 1% of the time, Pallas kernels for 0%

commit v1 on v0

v1 whole, which is shorter than its diff:
```python
import functools

import jax
import jax.numpy as jnp
from jax import lax
from jax.experimental import pallas as pl
from jax.experimental.pallas import tpu as pltpu
from jax.sharding import PartitionSpec as P

MESH = pl.DeviceIdType.MESH
F32 = jnp.float32
BF16 = jnp.bfloat16
ROWS = 1024
VMEM_BYTES = 56 << 20


def place():
    r, c = lax.axis_index("row"), lax.axis_index("col")
    return (c // 2) % 4, r // 2, r % 2, c // 8, c % 2


def device(x, y, zh, zl, k):
    return (y * 2 + zh, zl * 8 + x * 2 + k)


def remote(src, dst, send, recv, target):
    return pltpu.make_async_remote_copy(
        src_ref=src, dst_ref=dst, send_sem=send, recv_sem=recv, device_id=target, device_id_type=MESH
    )


def greet(partners):
    barrier = pltpu.get_barrier_semaphore()
    for partner in partners:
        pl.semaphore_signal(barrier, inc=1, device_id=partner, device_id_type=MESH)
    pl.semaphore_wait(barrier, len(partners))


class Sends:
    def __init__(self, send_sems):
        self.sems = send_sems
        self.started = []

    def start(self, src, dst, recv, target):
        copy = remote(src, dst, self.sems.at[len(self.started)], recv, target)
        copy.start()
        self.started.append(copy)

    def finish(self):
        for copy in self.started:
            copy.wait_send()


def arrived(ref, recv, me):
    remote(ref, ref, recv, recv, me).wait_recv()


def each_chunk(rows, step, body):
    def go(i, carry):
        body(pl.ds(pl.multiple_of(i * step, step), step))
        return carry

    lax.fori_loop(0, rows // step, go, 0)


def add_into(out, terms, rows, step=128):
    def body(at):
        total = out[at, :].astype(F32)
        for term in terms:
            total = total + term[at, :].astype(F32)
        out[at, :] = total.astype(out.dtype)

    each_chunk(rows, step, body)


G1_PIECES = 4
G1_ROWS = ROWS * 2 // G1_PIECES


def gather_row_kernel(x_ref, out_ref, local_sem, send_sems, z_sems, near_sems, far_sems):
    x, y, zh, zl, k = place()
    right, left = device(x, (y + 1) % 4, zh, zl, k), device(x, (y + 3) % 4, zh, zl, k)
    over = device(x, y, 1 - zh, zl, k)
    greet([right, left, over])
    sends = Sends(send_sems)
    own = y * 2 + zh
    half = G1_ROWS // 2
    per = G1_PIECES // 2

    def piece(yy, p, part=None):
        block = (yy % 4) * 2 + (zh if p < per else 1 - zh)
        start, size = (p % per) * G1_ROWS, G1_ROWS
        if part is not None:
            start, size = start + part * half, half
        return out_ref.at[block, pl.ds(start, size)]

    mine = pltpu.make_async_copy(x_ref, out_ref.at[own], local_sem)
    mine.start()
    for p in range(per):
        sends.start(x_ref.at[pl.ds(p * G1_ROWS, G1_ROWS)], piece(y, p), z_sems.at[p], over)
    for p in range(per):
        src = x_ref.at[pl.ds(p * G1_ROWS, G1_ROWS)]
        sends.start(src, piece(y, p), near_sems.at[p, 0], right)
        sends.start(src, piece(y, p), near_sems.at[p, 1], left)

    def spread(p):
        here = piece(y, p)
        arrived(here, z_sems.at[p - per], over)
        sends.start(here, here, near_sems.at[p, 0], right)
        sends.start(here, here, near_sems.at[p, 1], left)

    def forward(p):
        arrived(piece(y + 3, p), near_sems.at[p, 0], left)
        src = piece(y + 3, p, 0)
        sends.start(src, src, far_sems.at[p, 0], right)
        arrived(piece(y + 1, p), near_sems.at[p, 1], right)
        src = piece(y + 1, p, 1)
        sends.start(src, src, far_sems.at[p, 1], left)

    for p in range(per):
        forward(p)
        spread(per + p)
    for p in range(per):
        forward(per + p)
    for p in range(G1_PIECES):
        arrived(piece(y + 2, p, 0), far_sems.at[p, 0], left)
        arrived(piece(y + 2, p, 1), far_sems.at[p, 1], right)
    sends.finish()
    mine.wait()


def gather_row(features):
    return pl.pallas_call(
        gather_row_kernel,
        out_shape=jax.ShapeDtypeStruct((8, ROWS, 128), BF16),
        in_specs=[pl.BlockSpec(memory_space=pl.ANY)],
        out_specs=pl.BlockSpec(memory_space=pl.ANY),
        scratch_shapes=[
            pltpu.SemaphoreType.DMA,
            pltpu.SemaphoreType.DMA((G1_PIECES // 2 + 4 * G1_PIECES,)),
            pltpu.SemaphoreType.DMA((G1_PIECES // 2,)),
            pltpu.SemaphoreType.DMA((G1_PIECES, 2)),
            pltpu.SemaphoreType.DMA((G1_PIECES, 2)),
        ],
        compiler_params=pltpu.CompilerParams(
            collective_id=1, has_side_effects=True, vmem_limit_bytes=VMEM_BYTES
        ),
    )(features)


TURN = 4


def forward_kernel(rows_ref, cols_ref, live_ref, x_ref, w_ref, tiles_ref, out_ref, xv, proj, tiles, acc, sems):
    load_x = pltpu.make_async_copy(x_ref, xv, sems.at[0])
    load_t = pltpu.make_async_copy(tiles_ref, tiles, sems.at[1])
    load_x.start()
    load_t.start()

    def clear(i, carry):
        acc[pl.ds(i * 4, 4)] = jnp.zeros((4, 128, 128), BF16)
        return carry

    lax.fori_loop(0, 64, clear, 0)
    load_x.wait()
    weight = w_ref[...]

    def project(i, carry):
        block = xv[pl.ds(pl.multiple_of(i * 512, 512), 512), :]
        value = jnp.dot(block, weight, preferred_element_type=F32).astype(BF16)
        proj[pl.ds(i * 4, 4)] = value.reshape(4, 128, 128)
        return carry

    lax.fori_loop(0, 16, project, 0)
    load_t.wait()

    def turn(i, carry):
        products = []
        for u in range(TURN):
            s = i * TURN + u
            products.append(jnp.dot(tiles[s], proj[cols_ref[s]], preferred_element_type=F32))
        for u in range(TURN):
            b = rows_ref[i * TURN + u]
            acc[b] = (acc[b].astype(F32) + products[u]).astype(BF16)
        return carry

    lax.fori_loop(0, live_ref[0] // TURN, turn, 0)
    store = pltpu.make_async_copy(acc, out_ref, sems.at[2])
    store.start()
    store.wait()


def forward(rows, cols, live, x, weight, tiles):
    smem, vmem, anywhere = (pl.BlockSpec(memory_space=m) for m in (pltpu.SMEM, pltpu.VMEM, pl.ANY))
    return pl.pallas_call(
        forward_kernel,
        out_shape=jax.ShapeDtypeStruct((256, 128, 128), BF16),
        in_specs=[smem, smem, smem, anywhere, vmem, anywhere],
        out_specs=anywhere,
        scratch_shapes=[
            pltpu.VMEM((8 * ROWS, 128), BF16),
            pltpu.VMEM((64, 128, 128), BF16),
            pltpu.VMEM((64, 128, 128), BF16),
            pltpu.VMEM((256, 128, 128), BF16),
            pltpu.SemaphoreType.DMA((3,)),
        ],
        compiler_params=pltpu.CompilerParams(vmem_limit_bytes=VMEM_BYTES),
    )(rows, cols, live, x, weight, tiles)


ORDER = (2, 1, 3, 0)
HALF = ROWS // 2
H1, H2 = pl.ds(0, HALF), pl.ds(HALF, HALF)


def middle_kernel(
    part_ref, cot_ref, layer_ref, grows_ref,
    own, sib, s1, s2, zin, gown,
    load_sems, sib_sems, s1_sems, s2_sems, z_sems, send_sems,
    gz_sems, gnear_sems, gfar_sems, gsib_sems,
):
    x, y, zh, zl, k = place()
    me = device(x, y, zh, zl, k)
    right, left = device((x + 1) % 4, y, zh, zl, k), device((x + 3) % 4, y, zh, zl, k)
    sibling = device(x, y, zh, zl, 1 - k)
    along = [None] + [device(x, y, zh, (zl + j) % 4, k) for j in range(1, 4)]
    loads = {}
    for j in ORDER:
        for m in (2, 1, 3, 0):
            c = ((zl + j) % 4) * 8 + ((x + m) % 4) * 2 + k
            loads[j, m] = pltpu.make_async_copy(part_ref.at[c], own.at[j, m], load_sems.at[j, m])
            loads[j, m].start()
    greet([right, left, sibling] + along[1:])
    sends = Sends(send_sems)
    for j in ORDER:
        for m in (2, 1, 3, 0):
            c = ((zl + j) % 4) * 8 + ((x + m) % 4) * 2 + (1 - k)
            sends.start(part_ref.at[c], sib.at[j, m], sib_sems.at[j, m], sibling)

    def joined(j, m):
        loads[j, m].wait()
        arrived(sib.at[j, m], sib_sems.at[j, m], sibling)

    def step_a(j):
        joined(j, 2)
        add_into(own.at[j, 2], [sib.at[j, 2]], ROWS)
        sends.start(own.at[j, 2, H1], s1.at[j, 0], s1_sems.at[j, 0], right)
        sends.start(own.at[j, 2, H2], s1.at[j, 1], s1_sems.at[j, 1], left)

    def step_b(j):
        for m, side, near, far, target, source in ((1, 0, H1, H2, right, left), (3, 1, H2, H1, left, right)):
            joined(j, m)
            add_into(own.at[j, m, far], [sib.at[j, m, far]], HALF)
            arrived(s1.at[j, side], s1_sems.at[j, side], source)
            add_into(own.at[j, m, near], [sib.at[j, m, near], s1.at[j, side]], HALF)
            sends.start(own.at[j, m], s2.at[j, side], s2_sems.at[j, side], target)

    def step_c(j):
        joined(j, 0)
        arrived(s2.at[j, 0], s2_sems.at[j, 0], left)
        arrived(s2.at[j, 1], s2_sems.at[j, 1], right)
        if j:
            add_into(own.at[j, 0], [sib.at[j, 0], s2.at[j, 0], s2.at[j, 1]], ROWS)
            sends.start(own.at[j, 0], zin.at[j - 1], z_sems.at[j - 1], along[j])

    a, b, c_, d = ORDER
    step_a(a)
    step_a(b)
    step_b(a)
    step_a(c_)
    step_b(b)
    step_c(a)
    step_a(d)
    step_b(c_)
    step_c(b)
    step_b(d)
    step_c(c_)
    step_c(d)
    for j in range(1, 4):
        arrived(zin.at[j - 1], z_sems.at[j - 1], along[(4 - j) % 4])

    def finish(at):
        pre = own[0, 0, at, :].astype(F32)
        for term in (sib.at[0, 0], s2.at[0, 0], s2.at[0, 1], zin.at[0], zin.at[1], zin.at[2]):
            pre = pre + term[at, :].astype(F32)
        sigma = jax.nn.sigmoid(pre)
        layer_ref[at, :] = (pre * sigma).astype(BF16)
        slope = sigma * (1.0 + pre * (1.0 - sigma))
        gown[at, :] = (cot_ref[at, :].astype(F32) * slope).astype(BF16)

    each_chunk(ROWS, 128, finish)

    def block(j, m, part=None):
        c = ((zl + 4 - j) % 4) * 8 + ((x + m) % 4) * 2 + k
        return grows_ref.at[c] if part is None else grows_ref.at[c, (H1, H2)[part]]

    def other(j, m, part=None):
        c = ((zl + 4 - j) % 4) * 8 + ((x + m) % 4) * 2 + (1 - k)
        return grows_ref.at[c] if part is None else grows_ref.at[c, (H1, H2)[part]]

    mine = pltpu.make_async_copy(gown, block(0, 0), load_sems.at[0, 0])
    mine.start()
    for j in range(1, 4):
        sends.start(gown, block(0, 0), gz_sems.at[j - 1], along[j])

    def spread(j):
        src = gown
        if j:
            src = block(j, 0)
            arrived(src, gz_sems.at[j - 1], along[(4 - j) % 4])
        sends.start(src, block(j, 0), gnear_sems.at[j, 0], right)
        sends.start(src, block(j, 0), gnear_sems.at[j, 1], left)
        sends.start(src, block(j, 0), gsib_sems.at[j, 0], sibling)

    def relay(j):
        arrived(block(j, 3), gnear_sems.at[j, 0], left)
        sends.start(block(j, 3, 0), block(j, 3, 0), gfar_sems.at[j, 0], right)
        arrived(block(j, 1), gnear_sems.at[j, 1], right)
        sends.start(block(j, 1, 1), block(j, 1, 1), gfar_sems.at[j, 1], left)
        sends.start(block(j, 3), block(j, 3), gsib_sems.at[j, 1], sibling)
        sends.start(block(j, 1), block(j, 1), gsib_sems.at[j, 2], sibling)

    def share(j):
        arrived(block(j, 2, 0), gfar_sems.at[j, 0], left)
        sends.start(block(j, 2, 0), block(j, 2, 0), gsib_sems.at[j, 3], sibling)
        arrived(block(j, 2, 1), gfar_sems.at[j, 1], right)
        sends.start(block(j, 2, 1), block(j, 2, 1), gsib_sems.at[j, 4], sibling)

    a, b, c_, d = 0, 1, 3, 2
    spread(a)
    spread(b)
    relay(a)
    spread(c_)
    relay(b)
    share(a)
    spread(d)
    relay(c_)
    share(b)
    relay(d)
    share(c_)
    share(d)
    for j in range(4):
        arrived(other(j, 0), gsib_sems.at[j, 0], sibling)
        arrived(other(j, 3), gsib_sems.at[j, 1], sibling)
        arrived(other(j, 1), gsib_sems.at[j, 2], sibling)
        arrived(other(j, 2, 0), gsib_sems.at[j, 3], sibling)
        arrived(other(j, 2, 1), gsib_sems.at[j, 4], sibling)
    sends.finish()
    mine.wait()


def middle(part, cotangent):
    vmem, anywhere = (pl.BlockSpec(memory_space=m) for m in (pltpu.VMEM, pl.ANY))
    dma = pltpu.SemaphoreType.DMA
    return pl.pallas_call(
        middle_kernel,
        out_shape=(
            jax.ShapeDtypeStruct((ROWS, 128), BF16),
            jax.ShapeDtypeStruct((32, ROWS, 128), BF16),
        ),
        in_specs=[anywhere, vmem],
        out_specs=(vmem, anywhere),
        scratch_shapes=[
            pltpu.VMEM((4, 4, ROWS, 128), BF16),
            pltpu.VMEM((4, 4, ROWS, 128), BF16),
            pltpu.VMEM((4, 2, HALF, 128), BF16),
            pltpu.VMEM((4, 2, ROWS, 128), BF16),
            pltpu.VMEM((3, ROWS, 128), BF16),
            pltpu.VMEM((ROWS, 128), BF16),
            dma((4, 4)), dma((4, 4)), dma((4, 2)), dma((4, 2)), dma((3,)), dma((80,)),
            dma((3,)), dma((4, 2)), dma((4, 2)), dma((4, 5)),
        ],
        compiler_params=pltpu.CompilerParams(
            collective_id=2, has_side_effects=True, vmem_limit_bytes=VMEM_BYTES
        ),
    )(part, cotangent)


def backward_kernel(rows_ref, cols_ref, live_ref, g_ref, tiles_ref, out_ref, gv, tiles, acc, outv, sems, g_sems):
    load_t = pltpu.make_async_copy(tiles_ref, tiles, sems.at[0])
    load_t.start()
    live = live_ref[0]

    def fetch(s):
        return pltpu.make_async_copy(g_ref.at[rows_ref[s]], gv.at[s], g_sems.at[s])

    def begin(s, carry):
        fetch(s).start()
        return carry

    lax.fori_loop(0, live, begin, 0)

    def clear(i, carry):
        acc[pl.ds(i * 2, 2)] = jnp.zeros((2, 128, 128), F32)
        return carry

    lax.fori_loop(0, 32, clear, 0)
    load_t.wait()

    def turn(i, carry):
        products = []
        for u in range(TURN):
            s = i * TURN + u
            fetch(s).wait()
        for u in range(TURN):
            s = i * TURN + u
            products.append(
                lax.dot_general(tiles[s], gv[s], (((0,), (0,)), ((), ())), preferred_element_type=F32)
            )
        for u in range(TURN):
            b = cols_ref[i * TURN + u]
            acc[b] = acc[b] + products[u]
        return carry

    lax.fori_loop(0, live // TURN, turn, 0)

    def pack(i, carry):
        outv[pl.ds(i * 2, 2)] = acc[pl.ds(i * 2, 2)].astype(BF16)
        return carry

    lax.fori_loop(0, 32, pack, 0)
    store = pltpu.make_async_copy(outv, out_ref, sems.at[1])
    store.start()
    store.wait()


def backward(rows, cols, live, grows, tiles):
    smem, anywhere = (pl.BlockSpec(memory_space=m) for m in (pltpu.SMEM, pl.ANY))
    return pl.pallas_call(
        backward_kernel,
        out_shape=jax.ShapeDtypeStruct((64, 128, 128), BF16),
        in_specs=[smem, smem, smem, anywhere, anywhere],
        out_specs=anywhere,
        scratch_shapes=[
            pltpu.VMEM((64, 128, 128), BF16),
            pltpu.VMEM((64, 128, 128), BF16),
            pltpu.VMEM((64, 128, 128), F32),
            pltpu.VMEM((64, 128, 128), BF16),
            pltpu.SemaphoreType.DMA((2,)),
            pltpu.SemaphoreType.DMA((64,)),
        ],
        compiler_params=pltpu.CompilerParams(vmem_limit_bytes=VMEM_BYTES),
    )(rows, cols, live, grows, tiles)


PIECE = ROWS // 2
QUARTER = PIECE // 2
GROW = 16


def last_kernel(
    back_ref, x_ref, w_ref, gx_ref, gw_ref,
    own, xv, s1, s2, zin, gcore, gx4, gy4, gz8, gpart, final,
    load_sems, s1_sems, s2_sems, z_sems, send_sems,
    wcore_sems, wx_sems, wy_sems, wz_sems, wg_sems, wc_sems,
):
    x, y, zh, zl, k = place()
    right, left = device(x, (y + 1) % 4, zh, zl, k), device(x, (y + 3) % 4, zh, zl, k)
    over = device(x, y, 1 - zh, zl, k)
    sibling = device(x, y, zh, zl, 1 - k)
    xs = [None] + [device((x + i) % 4, y, zh, zl, k) for i in range(1, 4)]
    ys = [None] + [device(x, (y + i) % 4, zh, zl, k) for i in range(1, 4)]
    z = zh * 4 + zl

    def at_z(v):
        return device(x, y, v // 4, v % 4, k)

    zs = [None] + [at_z((z + i) % 8) for i in range(1, 8)]
    load = pltpu.make_async_copy(back_ref, own, load_sems.at[0])
    load.start()
    load_x = pltpu.make_async_copy(x_ref, xv, load_sems.at[1])
    load_x.start()
    greet([sibling] + xs[1:] + ys[1:] + zs[1:])
    sends = Sends(send_sems)

    def dest(m, t):
        return ((y + m) % 4) * 2 + (1 - zh if t == 0 else zh)

    def rows(q, part=None):
        if part is None:
            return pl.ds(q * PIECE, PIECE)
        return pl.ds(q * PIECE + part * QUARTER, QUARTER)

    pieces = [(0, 0), (0, 1), (1, 0), (1, 1)]
    for p, (t, q) in enumerate(pieces):
        sends.start(back_ref.at[dest(2, t), rows(q, 0)], s1.at[p, 0], s1_sems.at[p, 0], right)
        sends.start(back_ref.at[dest(2, t), rows(q, 1)], s1.at[p, 1], s1_sems.at[p, 1], left)
    load.wait()
    load_x.wait()

    def step_b(p):
        t, q = pieces[p]
        for m, side, target, source in ((1, 0, right, left), (3, 1, left, right)):
            arrived(s1.at[p, side], s1_sems.at[p, side], source)
            add_into(own.at[dest(m, t), rows(q, side)], [s1.at[p, side]], QUARTER)
            sends.start(own.at[dest(m, t), rows(q)], s2.at[p, side], s2_sems.at[p, side], target)

    def step_c(p):
        t, q = pieces[p]
        arrived(s2.at[p, 0], s2_sems.at[p, 0], left)
        arrived(s2.at[p, 1], s2_sems.at[p, 1], right)
        if t == 0:
            add_into(own.at[dest(0, t), rows(q)], [s2.at[p, 0], s2.at[p, 1]], PIECE)
            sends.start(own.at[dest(0, t), rows(q)], zin.at[q], z_sems.at[q], over)

    gpart[...] = jnp.zeros((128, 128), F32)

    def weight_grad(i, carry):
        gpart[...] += lax.dot_general(
            xv[i], own[i], (((0,), (0,)), ((), ())), preferred_element_type=F32
        )
        return carry

    lax.fori_loop(0, 8, weight_grad, 0)
    sends.start(gpart.at[pl.ds((1 - k) * 64, 64)], gcore, wcore_sems.at[0], sibling)
    step_b(0)
    step_b(1)
    arrived(gcore, wcore_sems.at[0], sibling)
    mine = pl.ds(k * 64, 64)
    gpart[mine, :] = gpart[mine, :] + gcore[...]
    for i in range(1, 4):
        at = pl.ds(k * 64 + ((x + i) % 4) * GROW, GROW)
        sends.start(gpart.at[at], gx4.at[i], wx_sems.at[i], xs[i])
    step_c(0)
    for i in range(1, 4):
        arrived(gx4.at[i], wx_sems.at[i], xs[4 - i])
    share = pl.ds(k * 64 + x * GROW, GROW)
    gx4[0] = gpart[share, :] + gx4[1] + gx4[2] + gx4[3]
    for i in range(1, 4):
        sends.start(gx4.at[0], gy4.at[i], wy_sems.at[i], ys[i])
    step_b(2)
    step_c(1)
    for i in range(1, 4):
        arrived(gy4.at[i], wy_sems.at[i], ys[4 - i])
    gy4[0] = gx4[0] + gy4[1] + gy4[2] + gy4[3]
    for i in range(1, 8):
        sends.start(gy4.at[0], gz8.at[i], wz_sems.at[i], zs[i])
    step_b(3)
    for i in range(1, 8):
        arrived(gz8.at[i], wz_sems.at[i], zs[8 - i])
    total = gy4[0]
    for i in range(1, 8):
        total = total + gz8[i]
    final[share, :] = total
    for i in range(1, 4):
        sends.start(final.at[share], final.at[share], wg_sems.at[i], xs[i])
    step_c(2)
    for i in range(1, 4):
        from_x = pl.ds(k * 64 + ((x + 4 - i) % 4) * GROW, GROW)
        arrived(final.at[from_x], wg_sems.at[i], xs[4 - i])
    sends.start(final.at[mine], final.at[mine], wc_sems.at[0], sibling)
    step_c(3)
    weight = w_ref[...]
    for q in range(2):
        arrived(zin.at[q], z_sems.at[q], over)
        p = 2 + q

        def output(at):
            value = own[dest(0, 1), pl.ds(q * PIECE + at.start, at.size), :].astype(F32)
            for term in (s2.at[p, 0], s2.at[p, 1], zin.at[q]):
                value = value + term[at, :].astype(F32)
            high = value.astype(BF16)
            low = (value - high.astype(F32)).astype(BF16)
            dims = (((1,), (1,)), ((), ()))
            result = lax.dot_general(high, weight, dims, preferred_element_type=F32)
            result = result + lax.dot_general(low, weight, dims, preferred_element_type=F32)
            gx_ref[pl.ds(q * PIECE + at.start, at.size), :] = result.astype(BF16)

        each_chunk(PIECE, 256, output)
    arrived(final.at[pl.ds((1 - k) * 64, 64)], wc_sems.at[0], sibling)
    gw_ref[...] = final[...]
    sends.finish()


def last(back, x, weight):
    vmem, anywhere = (pl.BlockSpec(memory_space=m) for m in (pltpu.VMEM, pl.ANY))
    dma = pltpu.SemaphoreType.DMA
    return pl.pallas_call(
        last_kernel,
        out_shape=(jax.ShapeDtypeStruct((ROWS, 128), BF16), jax.ShapeDtypeStruct((128, 128), F32)),
        in_specs=[anywhere, anywhere, vmem],
        out_specs=(vmem, vmem),
        scratch_shapes=[
            pltpu.VMEM((8, ROWS, 128), BF16),
            pltpu.VMEM((8, ROWS, 128), BF16),
            pltpu.VMEM((4, 2, QUARTER, 128), BF16),
            pltpu.VMEM((4, 2, PIECE, 128), BF16),
            pltpu.VMEM((2, PIECE, 128), BF16),
            pltpu.VMEM((64, 128), F32),
            pltpu.VMEM((4, GROW, 128), F32),
            pltpu.VMEM((4, GROW, 128), F32),
            pltpu.VMEM((8, GROW, 128), F32),
            pltpu.VMEM((128, 128), F32),
            pltpu.VMEM((128, 128), F32),
            dma((2,)), dma((4, 2)), dma((4, 2)), dma((2,)), dma((40,)),
            dma((1,)), dma((4,)), dma((4,)), dma((8,)), dma((4,)), dma((1,)),
        ],
        compiler_params=pltpu.CompilerParams(
            collective_id=3, has_side_effects=True, vmem_limit_bytes=VMEM_BYTES
        ),
    )(back, x, weight)


def shards(features, weight, tile_values, tile_rows, tile_cols, tile_live, cotangent):
    tiles = tile_values[0, 0]
    rows = tile_rows[0, 0]
    cols = tile_cols[0, 0]
    live = tile_live[0]
    gathered = gather_row(features)
    part = forward(rows, cols, live, gathered.reshape(8 * ROWS, 128), weight, tiles)
    layer_out, grows = middle(part.reshape(32, ROWS, 128), cotangent)
    back = backward(rows, cols, live, grows.reshape(256, 128, 128), tiles)
    grad_x, grad_w = last(back.reshape(8, ROWS, 128), gathered, weight)
    return (layer_out, grad_x, grad_w)


def solution(mesh):
    in_specs = (
        P(("col", "row"), None),
        P(),
        P("row", "col", None, None, None),
        P("row", "col", None),
        P("row", "col", None),
        P("row", "col"),
        P(("row", "col"), None),
    )
    out_specs = (P(("row", "col"), None), P(("col", "row"), None), P())
    return jax.shard_map(shards, mesh=mesh, in_specs=in_specs, out_specs=out_specs, check_vma=False)
```

time: 727 us -> 192 us (0.26)
  waiting for transfers between devices: 628 us -> 0 us
  Pallas kernels: 0 us -> 187 us
  other arithmetic: 42.8 us -> 0 us
  local copies, waits for them, and re-layouts: 28.7 us -> 3.85 us
  between operations: 13.8 us -> 1.33 us
  matrix products: 12 us -> 0 us
    reduce_scatter x2 -> x0, waiting for transfers between devices: 241 us -> none  [the longest x1 149 us: shards(): lax.psum_scatter(partial_value.reshape(-1, width).astype(jnp.bfloat16), '...]
    psum x1 -> x0, waiting for transfers between devices: 238 us -> none  [shards(): grad_w = lax.psum(weight_term, ('row', 'col'))]
    pallas_call x0 -> x5, Pallas kernels: none -> 187 us  [the longest x1 99.4 us: middle(): pl.pallas_call(middle_kernel, out_shape=(jax.ShapeDtypeStruct((ROWS, 128)...]
    all_gather x2 -> x0, waiting for transfers between devices: 149 us -> none  [the longest x1 80.1 us: shards(): projected = lax.all_gather(own_proj, 'row', axis=0, tiled=True)]
    scatter-add x4 -> x0, other arithmetic: 24.8 us -> none  [the longest x2 12.5 us: advance(): return accumulated.at[target_piece].add(product)]
    convert_element_type x3 -> x0, other arithmetic: 15.1 us -> none  [the longest x1 9.19 us: shards(): partial_value.reshape(-1, width).astype(jnp.bfloat16)]
    gather x4 -> x0, local copies, waits for them, and re-layouts: 12.9 us -> none  [the longest x2 8.26 us: advance(): source[row_piece]]
    dot_general x7 -> x0, matrix products: 12 us -> none  [the longest x2 3.31 us: advance(): jnp.einsum('tij,tif->tjf', piece, source[row_piece], preferred_element_ty...]
  transfers between devices with their start and end apart: 5 -> 0, of which waited for: 5 -> 0; matrix products, arithmetic and copies ran while one was open for 1% -> 0% of each run, Pallas kernels for 0% -> 0%
where the time goes in v1:
time: 192 us
  Pallas kernels  187 us (97%)
  local copies, waits for them, and re-layouts  3.85 us (2%)
    pallas_call x1, Pallas kernels, middle(): pl.pallas_call(middle_kernel, out_shape=(jax.ShapeDtypeStruct((ROWS, 128)...  99.4 us
    pallas_call x1, Pallas kernels, last(): pl.pallas_call(last_kernel, out_shape=(jax.ShapeDtypeStruct((ROWS, 128),...  42.8 us
    pallas_call x1, Pallas kernels, gather_row(): pl.pallas_call(gather_row_kernel, out_shape=jax.ShapeDtypeStruct((8, ROWS...  28.3 us
    pallas_call x1, Pallas kernels, forward(): pl.pallas_call(forward_kernel, out_shape=jax.ShapeDtypeStruct((256, 128,...  9.95 us
    pallas_call x1, Pallas kernels, backward(): pl.pallas_call(backward_kernel, out_shape=jax.ShapeDtypeStruct((64, 128,...  6.49 us
    unnamed x5, local copies, waits for them, and re-layouts  3.85 us

profile of v1, /device:TPU:1, one launch (start us, length us, event | category | flops | bytes accessed | tf_op | source)
XLA Modules:
  0.0 192.1 jit_solution(12647653028985797347)
XLA Ops:
  1.3 28.3 %shard_map.94.x_ref = bf16[8,1024,128]{2,1,0:T(8,128)(2,1)} custom-call(bf16[1024,128]{1,0:T(8,128)(2,1)} %x_ref.1), custom_call_target="tpu_custom_call" | custom-call | tf_op jit(solution)/shard_map/pallas_call | solution.py:133
  29.6 9.9 %shard_map.95 = bf16[256,128,128]{2,1,0:T(8,128)(2,1)} custom-call(s32[64]{0:T(128)} %bitcast.16, s32[64]{0:T(128)} %bitcast.18, s32[1]{0:T(128)} %bitcast.8.live_ref, bf16[8192,128]{1,0:T(8,128)(2,1)} %bitcast.11, bf16[128,128]{1,0:T(8,128)(2,1)} %w_ref.3, bf16[64,128,128]{2,1,0:T(8,128)(2,1)} %bitcast.12), custom_call_target="tpu_custom_call" | custom-call | tf_op jit(solution)/shard_map/pallas_call | solution.py:195
  39.6 99.4 %shard_map.96 = (bf16[1024,128]{1,0:T(8,128)(2,1)}, bf16[32,1024,128]{2,1,0:T(8,128)(2,1)}) custom-call(bf16[32,1024,128]{2,1,0:T(8,128)(2,1)} %bitcast.10, bf16[1024,128]{1,0:T(8,128)(2,1)} %cot_ref.1), custom_call_target="tpu_custom_call" | custom-call | tf_op jit(solution)/shard_map/pallas_call | solution.py:355
  139.0 6.5 %shard_map.97 = bf16[64,128,128]{2,1,0:T(8,128)(2,1)} custom-call(s32[64]{0:T(128)} %bitcast.17, s32[64]{0:T(128)} %bitcast.19, s32[1]{0:T(128)} %bitcast.9.live_ref, bf16[256,128,128]{2,1,0:T(8,128)(2,1)} %bitcast.15, bf16[64,128,128]{2,1,0:T(8,128)(2,1)} %bitcast.13), custom_call_target="tpu_custom_call" | custom-call | tf_op jit(solution)/shard_map/pallas_call | solution.py:429
  145.5 0.0 copy-start
  145.5 42.8 %shard_map.98 = (bf16[1024,128]{1,0:T(8,128)(2,1)}, f32[128,128]{1,0:T(8,128)}) custom-call(bf16[8,1024,128]{2,1,0:T(8,128)(2,1)} %bitcast.14, bf16[8,1024,128]{2,1,0:T(8,128)(2,1)} %shard_map.94.x_ref, bf16[128,128]{1,0:T(8,128)(2,1)} %w_ref.3), custom_call_target="tpu_custom_call" | custom-call | tf_op jit(solution)/shard_map/pallas_call | solution.py:578
  188.3 0.0 copy-done
  188.3 0.7 copy.14
  189.0 1.7 copy.15
  190.7 1.5 copy.16
Async XLA Ops:
  145.5 42.8 %copy-start = (bf16[1024,128]{1,0:T(8,128)(2,1)S(1)}, bf16[1024,128]{1,0:T(8,128)(2,1)}, u32[]{:S(2)}) copy-start(bf16[1024,128]{1,0:T(8,128)(2,1)} %get-tuple-element.14) | copy-start | bytes 786436

commit v2 on v1

v2 whole, which is shorter than its diff:
```python
import functools

import jax
import jax.numpy as jnp
from jax import lax
from jax.experimental import pallas as pl
from jax.experimental.pallas import tpu as pltpu
from jax.sharding import PartitionSpec as P

MESH = pl.DeviceIdType.MESH
F32 = jnp.float32
BF16 = jnp.bfloat16
ROWS = 1024
VMEM_BYTES = 56 << 20


def place():
    r, c = lax.axis_index("row"), lax.axis_index("col")
    return (c // 2) % 4, r // 2, r % 2, c // 8, c % 2


def device(x, y, zh, zl, k):
    return (y * 2 + zh, zl * 8 + x * 2 + k)


def remote(src, dst, send, recv, target):
    return pltpu.make_async_remote_copy(
        src_ref=src, dst_ref=dst, send_sem=send, recv_sem=recv, device_id=target, device_id_type=MESH
    )


def greet(partners):
    barrier = pltpu.get_barrier_semaphore()
    for partner in partners:
        pl.semaphore_signal(barrier, inc=1, device_id=partner, device_id_type=MESH)
    pl.semaphore_wait(barrier, len(partners))


class Sends:
    def __init__(self, send_sems):
        self.sems = send_sems
        self.started = []

    def start(self, src, dst, recv, target):
        copy = remote(src, dst, self.sems.at[len(self.started)], recv, target)
        copy.start()
        self.started.append(copy)

    def finish(self):
        for copy in self.started:
            copy.wait_send()


def arrived(ref, recv, me):
    remote(ref, ref, recv, recv, me).wait_recv()


def each_chunk(rows, step, body):
    def go(i, carry):
        body(pl.ds(pl.multiple_of(i * step, step), step))
        return carry

    lax.fori_loop(0, rows // step, go, 0)


def add_into(out, terms, rows, step=128):
    def body(at):
        total = out[at, :].astype(F32)
        for term in terms:
            total = total + term[at, :].astype(F32)
        out[at, :] = total.astype(out.dtype)

    each_chunk(rows, step, body)


G1 = ((0, 0, 512), (0, 512, 512), (1, 0, 256), (1, 256, 256), (1, 512, 256), (1, 768, 256))
G1_OVER = (2, 3, 4, 5)
G1_ORDER = (("far", 0), ("near", 2), ("far", 1), ("near", 3), ("far", 2), ("near", 4), ("far", 3), ("near", 5), ("far", 4), ("far", 5))


def gather_row_kernel(x_ref, out_ref, local_sem, send_sems, z_sems, near_sems, far_sems):
    x, y, zh, zl, k = place()
    right, left = device(x, (y + 1) % 4, zh, zl, k), device(x, (y + 3) % 4, zh, zl, k)
    over = device(x, y, 1 - zh, zl, k)
    greet([right, left, over])
    sends = Sends(send_sems)
    own = y * 2 + zh

    def piece(yy, p, part=None):
        side, start, size = G1[p]
        block = (yy % 4) * 2 + (1 - zh if side else zh)
        if part is not None:
            size = size // 2
            start = start + part * size
        return out_ref.at[block, pl.ds(start, size)]

    mine = pltpu.make_async_copy(x_ref, out_ref.at[own], local_sem)
    for p in G1_OVER:
        _, start, size = G1[p]
        rows = pl.ds(start, size)
        sends.start(x_ref.at[rows], out_ref.at[own, rows], z_sems.at[p], over)
    for p in (0, 1):
        _, start, size = G1[p]
        src = x_ref.at[pl.ds(start, size)]
        sends.start(src, piece(y, p), near_sems.at[p, 0], right)
        sends.start(src, piece(y, p), near_sems.at[p, 1], left)
    mine.start()

    def near(p):
        here = piece(y, p)
        arrived(here, z_sems.at[p], over)
        sends.start(here, here, near_sems.at[p, 0], right)
        sends.start(here, here, near_sems.at[p, 1], left)

    def far(p):
        arrived(piece(y + 3, p), near_sems.at[p, 0], left)
        src = piece(y + 3, p, 0)
        sends.start(src, src, far_sems.at[p, 0], right)
        arrived(piece(y + 1, p), near_sems.at[p, 1], right)
        src = piece(y + 1, p, 1)
        sends.start(src, src, far_sems.at[p, 1], left)

    for what, p in G1_ORDER:
        (near if what == "near" else far)(p)
    for p in range(len(G1)):
        arrived(piece(y + 2, p, 0), far_sems.at[p, 0], left)
        arrived(piece(y + 2, p, 1), far_sems.at[p, 1], right)
    sends.finish()
    mine.wait()


def gather_row(features):
    n = len(G1)
    return pl.pallas_call(
        gather_row_kernel,
        out_shape=jax.ShapeDtypeStruct((8, ROWS, 128), BF16),
        in_specs=[pl.BlockSpec(memory_space=pl.ANY)],
        out_specs=pl.BlockSpec(memory_space=pl.ANY),
        scratch_shapes=[
            pltpu.SemaphoreType.DMA,
            pltpu.SemaphoreType.DMA((len(G1_OVER) + 4 * n,)),
            pltpu.SemaphoreType.DMA((n,)),
            pltpu.SemaphoreType.DMA((n, 2)),
            pltpu.SemaphoreType.DMA((n, 2)),
        ],
        compiler_params=pltpu.CompilerParams(
            collective_id=1, has_side_effects=True, vmem_limit_bytes=VMEM_BYTES
        ),
    )(features)


TURN = 4


def forward_kernel(rows_ref, cols_ref, live_ref, x_ref, w_ref, tiles_ref, out_ref, xv, proj, tiles, acc, sems):
    load_x = pltpu.make_async_copy(x_ref, xv, sems.at[0])
    load_t = pltpu.make_async_copy(tiles_ref, tiles, sems.at[1])
    load_x.start()
    load_t.start()

    def clear(i, carry):
        acc[pl.ds(i * 4, 4)] = jnp.zeros((4, 128, 128), BF16)
        return carry

    lax.fori_loop(0, 64, clear, 0)
    load_x.wait()
    weight = w_ref[...]

    def project(i, carry):
        block = xv[pl.ds(pl.multiple_of(i * 512, 512), 512), :]
        value = jnp.dot(block, weight, preferred_element_type=F32).astype(BF16)
        proj[pl.ds(i * 4, 4)] = value.reshape(4, 128, 128)
        return carry

    lax.fori_loop(0, 16, project, 0)
    load_t.wait()

    def turn(i, carry):
        products = []
        for u in range(TURN):
            s = i * TURN + u
            products.append(jnp.dot(tiles[s], proj[cols_ref[s]], preferred_element_type=F32))
        for u in range(TURN):
            b = rows_ref[i * TURN + u]
            acc[b] = (acc[b].astype(F32) + products[u]).astype(BF16)
        return carry

    lax.fori_loop(0, live_ref[0] // TURN, turn, 0)
    store = pltpu.make_async_copy(acc, out_ref, sems.at[2])
    store.start()
    store.wait()


def forward(rows, cols, live, x, weight, tiles):
    smem, vmem, anywhere = (pl.BlockSpec(memory_space=m) for m in (pltpu.SMEM, pltpu.VMEM, pl.ANY))
    return pl.pallas_call(
        forward_kernel,
        out_shape=jax.ShapeDtypeStruct((256, 128, 128), BF16),
        in_specs=[smem, smem, smem, anywhere, vmem, anywhere],
        out_specs=anywhere,
        scratch_shapes=[
            pltpu.VMEM((8 * ROWS, 128), BF16),
            pltpu.VMEM((64, 128, 128), BF16),
            pltpu.VMEM((64, 128, 128), BF16),
            pltpu.VMEM((256, 128, 128), BF16),
            pltpu.SemaphoreType.DMA((3,)),
        ],
        compiler_params=pltpu.CompilerParams(vmem_limit_bytes=VMEM_BYTES),
    )(rows, cols, live, x, weight, tiles)


HALF = ROWS // 2
QUARTER = ROWS // 4
NEEDED = (
    (2, 2), (1, 2), (3, 2), (2, 1), (2, 3), (0, 2), (1, 1), (1, 3),
    (2, 0), (3, 1), (3, 3), (1, 0), (0, 1), (0, 3), (3, 0), (0, 0),
)
MIDDLE_ORDER = (
    ("a", 2, 0), ("a", 1, 0), ("a", 3, 0), ("b", 2, 0), ("a", 0, 0), ("b", 1, 0), ("a", 2, 1), ("b", 3, 0),
    ("c", 2, 0), ("a", 1, 1), ("b", 0, 0), ("c", 1, 0), ("a", 3, 1), ("b", 2, 1), ("c", 3, 0), ("a", 0, 1),
    ("b", 1, 1), ("c", 0, 0), ("end", 0, 0), ("b", 3, 1), ("c", 2, 1), ("b", 0, 1), ("near", 0, 0),
    ("c", 1, 1), ("near", 1, 0), ("c", 3, 1), ("near", 3, 0), ("c", 0, 1), ("end", 0, 1),
    ("near", 0, 1), ("far", 0, 0), ("far", 1, 0), ("near", 2, 0), ("far", 3, 0), ("near", 1, 1), ("share", 0, 0),
    ("share", 1, 0), ("far", 0, 1), ("near", 3, 1), ("far", 2, 0), ("share", 3, 0), ("far", 1, 1), ("near", 2, 1),
    ("share", 2, 0), ("share", 0, 1), ("far", 3, 1), ("share", 1, 1), ("far", 2, 1), ("share", 3, 1), ("share", 2, 1),
)


def middle_kernel(
    part_ref, cot_ref, layer_ref, grows_ref,
    own, sib, s1, s2, zin, gown,
    load_sems, sib_sems, s1_sems, s2_sems, z_sems, send_sems,
    gz_sems, gnear_sems, gfar_sems, gsib_sems, mine_sems,
):
    x, y, zh, zl, k = place()
    right, left = device((x + 1) % 4, y, zh, zl, k), device((x + 3) % 4, y, zh, zl, k)
    sibling = device(x, y, zh, zl, 1 - k)
    along = [None] + [device(x, y, zh, (zl + j) % 4, k) for j in range(1, 4)]
    halves = (pl.ds(0, HALF), pl.ds(HALF, HALF))
    loads = {}
    for j, m in NEEDED:
        c = ((zl + j) % 4) * 8 + ((x + m) % 4) * 2 + k
        loads[j, m] = pltpu.make_async_copy(part_ref.at[c], own.at[j, m], load_sems.at[j, m])
        loads[j, m].start()
    greet([right, left, sibling] + along[1:])
    sends = Sends(send_sems)
    for q in range(2):
        for j, m in NEEDED:
            c = ((zl + j) % 4) * 8 + ((x + m) % 4) * 2 + (1 - k)
            sends.start(part_ref.at[c, halves[q]], sib.at[j, m, halves[q]], sib_sems.at[j, m, q], sibling)
    loaded = set()

    def joined(j, m, q):
        if (j, m) not in loaded:
            loads[j, m].wait()
            loaded.add((j, m))
        arrived(sib.at[j, m, halves[q]], sib_sems.at[j, m, q], sibling)

    def quarters(q):
        return pl.ds(q * HALF, QUARTER), pl.ds(q * HALF + QUARTER, QUARTER)

    def step_a(j, q):
        joined(j, 2, q)
        add_into(own.at[j, 2, halves[q]], [sib.at[j, 2, halves[q]]], HALF)
        first, second = quarters(q)
        sends.start(own.at[j, 2, first], s1.at[q, j, 0], s1_sems.at[q, j, 0], right)
        sends.start(own.at[j, 2, second], s1.at[q, j, 1], s1_sems.at[q, j, 1], left)

    def step_b(j, q):
        first, second = quarters(q)
        for m, side, near, far, target, source in ((1, 0, first, second, right, left), (3, 1, second, first, left, right)):
            joined(j, m, q)
            add_into(own.at[j, m, far], [sib.at[j, m, far]], QUARTER)
            arrived(s1.at[q, j, side], s1_sems.at[q, j, side], source)
            add_into(own.at[j, m, near], [sib.at[j, m, near], s1.at[q, j, side]], QUARTER)
            sends.start(own.at[j, m, halves[q]], s2.at[q, j, side], s2_sems.at[q, j, side], target)

    def step_c(j, q):
        joined(j, 0, q)
        arrived(s2.at[q, j, 0], s2_sems.at[q, j, 0], left)
        arrived(s2.at[q, j, 1], s2_sems.at[q, j, 1], right)
        if j:
            add_into(own.at[j, 0, halves[q]], [sib.at[j, 0, halves[q]], s2.at[q, j, 0], s2.at[q, j, 1]], HALF)
            sends.start(own.at[j, 0, halves[q]], zin.at[q, j - 1], z_sems.at[q, j - 1], along[j])

    def block(j, m, q, part=None):
        c = ((zl + 4 - j) % 4) * 8 + ((x + m) % 4) * 2 + k
        return grows_ref.at[c, halves[q] if part is None else quarters(q)[part]]

    def other(j, m, q, part=None):
        c = ((zl + 4 - j) % 4) * 8 + ((x + m) % 4) * 2 + (1 - k)
        return grows_ref.at[c, halves[q] if part is None else quarters(q)[part]]

    mine = []

    def end(_, q):
        for j in range(1, 4):
            arrived(zin.at[q, j - 1], z_sems.at[q, j - 1], along[4 - j])
        base = q * HALF

        def finish(at):
            here = pl.ds(base + at.start, at.size)
            pre = own[0, 0, here, :].astype(F32) + sib[0, 0, here, :].astype(F32)
            for term in (s2.at[q, 0, 0], s2.at[q, 0, 1], zin.at[q, 0], zin.at[q, 1], zin.at[q, 2]):
                pre = pre + term[at, :].astype(F32)
            sigma = jax.nn.sigmoid(pre)
            layer_ref[here, :] = (pre * sigma).astype(BF16)
            slope = sigma * (1.0 + pre * (1.0 - sigma))
            gown[here, :] = (cot_ref[here, :].astype(F32) * slope).astype(BF16)

        each_chunk(HALF, 128, finish)
        src = gown.at[halves[q]]
        for j in (1, 3, 2):
            sends.start(src, block(0, 0, q), gz_sems.at[q, j - 1], along[j])
        mine.append(pltpu.make_async_copy(src, block(0, 0, q), mine_sems.at[q]))
        mine[-1].start()

    def near(j, q):
        src = gown.at[halves[q]]
        if j:
            src = block(j, 0, q)
            arrived(src, gz_sems.at[q, j - 1], along[4 - j])
        sends.start(src, block(j, 0, q), gnear_sems.at[q, j, 0], right)
        sends.start(src, block(j, 0, q), gnear_sems.at[q, j, 1], left)
        sends.start(src, block(j, 0, q), gsib_sems.at[q, j, 0], sibling)

    def far(j, q):
        arrived(block(j, 3, q), gnear_sems.at[q, j, 0], left)
        sends.start(block(j, 3, q, 0), block(j, 3, q, 0), gfar_sems.at[q, j, 0], right)
        arrived(block(j, 1, q), gnear_sems.at[q, j, 1], right)
        sends.start(block(j, 1, q, 1), block(j, 1, q, 1), gfar_sems.at[q, j, 1], left)
        sends.start(block(j, 3, q), block(j, 3, q), gsib_sems.at[q, j, 1], sibling)
        sends.start(block(j, 1, q), block(j, 1, q), gsib_sems.at[q, j, 2], sibling)

    def share(j, q):
        arrived(block(j, 2, q, 0), gfar_sems.at[q, j, 0], left)
        sends.start(block(j, 2, q, 0), block(j, 2, q, 0), gsib_sems.at[q, j, 3], sibling)
        arrived(block(j, 2, q, 1), gfar_sems.at[q, j, 1], right)
        sends.start(block(j, 2, q, 1), block(j, 2, q, 1), gsib_sems.at[q, j, 4], sibling)

    steps = {"a": step_a, "b": step_b, "c": step_c, "end": end, "near": near, "far": far, "share": share}
    for name, j, q in MIDDLE_ORDER:
        steps[name](j, q)
    for q in range(2):
        for j in range(4):
            arrived(other(j, 0, q), gsib_sems.at[q, j, 0], sibling)
            arrived(other(j, 3, q), gsib_sems.at[q, j, 1], sibling)
            arrived(other(j, 1, q), gsib_sems.at[q, j, 2], sibling)
            arrived(other(j, 2, q, 0), gsib_sems.at[q, j, 3], sibling)
            arrived(other(j, 2, q, 1), gsib_sems.at[q, j, 4], sibling)
    sends.finish()
    for copy in mine:
        copy.wait()


def middle(part, cotangent):
    vmem, anywhere = (pl.BlockSpec(memory_space=m) for m in (pltpu.VMEM, pl.ANY))
    dma = pltpu.SemaphoreType.DMA
    return pl.pallas_call(
        middle_kernel,
        out_shape=(
            jax.ShapeDtypeStruct((ROWS, 128), BF16),
            jax.ShapeDtypeStruct((32, ROWS, 128), BF16),
        ),
        in_specs=[anywhere, vmem],
        out_specs=(vmem, anywhere),
        scratch_shapes=[
            pltpu.VMEM((4, 4, ROWS, 128), BF16),
            pltpu.VMEM((4, 4, ROWS, 128), BF16),
            pltpu.VMEM((2, 4, 2, QUARTER, 128), BF16),
            pltpu.VMEM((2, 4, 2, HALF, 128), BF16),
            pltpu.VMEM((2, 3, HALF, 128), BF16),
            pltpu.VMEM((ROWS, 128), BF16),
            dma((4, 4)), dma((4, 4, 2)), dma((2, 4, 2)), dma((2, 4, 2)), dma((2, 3)), dma((160,)),
            dma((2, 3)), dma((2, 4, 2)), dma((2, 4, 2)), dma((2, 4, 5)), dma((2,)),
        ],
        compiler_params=pltpu.CompilerParams(
            collective_id=2, has_side_effects=True, vmem_limit_bytes=VMEM_BYTES
        ),
    )(part, cotangent)


def backward_kernel(rows_ref, cols_ref, live_ref, g_ref, tiles_ref, out_ref, gv, tiles, acc, outv, sems, g_sems):
    load_t = pltpu.make_async_copy(tiles_ref, tiles, sems.at[0])
    load_t.start()
    live = live_ref[0]

    def fetch(s):
        return pltpu.make_async_copy(g_ref.at[rows_ref[s]], gv.at[s], g_sems.at[s])

    def begin(s, carry):
        fetch(s).start()
        return carry

    lax.fori_loop(0, live, begin, 0)

    def clear(i, carry):
        acc[pl.ds(i * 2, 2)] = jnp.zeros((2, 128, 128), F32)
        return carry

    lax.fori_loop(0, 32, clear, 0)
    load_t.wait()

    def turn(i, carry):
        products = []
        for u in range(TURN):
            s = i * TURN + u
            fetch(s).wait()
        for u in range(TURN):
            s = i * TURN + u
            products.append(
                lax.dot_general(tiles[s], gv[s], (((0,), (0,)), ((), ())), preferred_element_type=F32)
            )
        for u in range(TURN):
            b = cols_ref[i * TURN + u]
            acc[b] = acc[b] + products[u]
        return carry

    lax.fori_loop(0, live // TURN, turn, 0)

    def pack(i, carry):
        outv[pl.ds(i * 2, 2)] = acc[pl.ds(i * 2, 2)].astype(BF16)
        return carry

    lax.fori_loop(0, 32, pack, 0)
    store = pltpu.make_async_copy(outv, out_ref, sems.at[1])
    store.start()
    store.wait()


def backward(rows, cols, live, grows, tiles):
    smem, anywhere = (pl.BlockSpec(memory_space=m) for m in (pltpu.SMEM, pl.ANY))
    return pl.pallas_call(
        backward_kernel,
        out_shape=jax.ShapeDtypeStruct((64, 128, 128), BF16),
        in_specs=[smem, smem, smem, anywhere, anywhere],
        out_specs=anywhere,
        scratch_shapes=[
            pltpu.VMEM((64, 128, 128), BF16),
            pltpu.VMEM((64, 128, 128), BF16),
            pltpu.VMEM((64, 128, 128), F32),
            pltpu.VMEM((64, 128, 128), BF16),
            pltpu.SemaphoreType.DMA((2,)),
            pltpu.SemaphoreType.DMA((64,)),
        ],
        compiler_params=pltpu.CompilerParams(vmem_limit_bytes=VMEM_BYTES),
    )(rows, cols, live, grows, tiles)


GROW = 16
PIECES = ((0, 0, 256), (0, 256, 256), (0, 512, 256), (0, 768, 256), (1, 0, 512), (1, 512, 512))
LAST_ORDER = (
    ("wg",), ("b", 0), ("b", 1), ("b", 2), ("b", 3), ("wx",), ("c", 0), ("wy",), ("a", 4), ("c", 1), ("a", 5),
    ("c", 2), ("c", 3), ("wz",), ("b", 4), ("b", 5), ("ws",), ("c", 4), ("wc",), ("c", 5),
)


def last_kernel(
    back_ref, x_ref, w_ref, gx_ref, gw_ref,
    own, xv, s1, s2, zin, gcore, gx4, gy4, gz8, gpart, final,
    load_sems, s1_sems, s2_sems, z_sems, send_sems,
    wcore_sems, wx_sems, wy_sems, wz_sems, wg_sems, wc_sems,
):
    x, y, zh, zl, k = place()
    right, left = device(x, (y + 1) % 4, zh, zl, k), device(x, (y + 3) % 4, zh, zl, k)
    over = device(x, y, 1 - zh, zl, k)
    sibling = device(x, y, zh, zl, 1 - k)
    xs = [None] + [device((x + i) % 4, y, zh, zl, k) for i in range(1, 4)]
    ys = [None] + [device(x, (y + i) % 4, zh, zl, k) for i in range(1, 4)]
    z = zh * 4 + zl

    def at_z(v):
        return device(x, y, v // 4, v % 4, k)

    zs = [None] + [at_z((z + i) % 8) for i in range(1, 8)]
    load = pltpu.make_async_copy(back_ref, own, load_sems.at[0])
    load.start()
    load_x = pltpu.make_async_copy(x_ref, xv, load_sems.at[1])
    load_x.start()
    greet([sibling] + xs[1:] + ys[1:] + zs[1:])
    sends = Sends(send_sems)

    def dest(m, p):
        return ((y + m) % 4) * 2 + (zh if PIECES[p][0] else 1 - zh)

    def rows(p, part=None):
        _, start, size = PIECES[p]
        if part is None:
            return pl.ds(start, size)
        return pl.ds(start + part * (size // 2), size // 2)

    def near(p, side):
        return s1.at[p, side, pl.ds(0, PIECES[p][2] // 2)]

    def far(p, side):
        return s2.at[p, side, pl.ds(0, PIECES[p][2])]

    def step_a(p):
        sends.start(back_ref.at[dest(2, p), rows(p, 0)], near(p, 0), s1_sems.at[p, 0], right)
        sends.start(back_ref.at[dest(2, p), rows(p, 1)], near(p, 1), s1_sems.at[p, 1], left)

    def step_b(p):
        for m, side, target, source in ((1, 0, right, left), (3, 1, left, right)):
            arrived(near(p, side), s1_sems.at[p, side], source)
            add_into(own.at[dest(m, p), rows(p, side)], [near(p, side)], PIECES[p][2] // 2)
            sends.start(own.at[dest(m, p), rows(p)], far(p, side), s2_sems.at[p, side], target)

    def step_c(p):
        arrived(far(p, 0), s2_sems.at[p, 0], left)
        arrived(far(p, 1), s2_sems.at[p, 1], right)
        if PIECES[p][0] == 0:
            add_into(own.at[dest(0, p), rows(p)], [far(p, 0), far(p, 1)], PIECES[p][2])
            sends.start(own.at[dest(0, p), rows(p)], zin.at[rows(p)], z_sems.at[p], over)

    mine = pl.ds(k * 64, 64)
    theirs = pl.ds((1 - k) * 64, 64)
    share = pl.ds(k * 64 + x * GROW, GROW)

    def weight_grad():
        load.wait()
        load_x.wait()
        gpart[...] = jnp.zeros((128, 128), F32)

        def block(i, carry):
            gpart[...] += lax.dot_general(
                xv[i], own[i], (((0,), (0,)), ((), ())), preferred_element_type=F32
            )
            return carry

        lax.fori_loop(0, 8, block, 0)
        sends.start(gpart.at[theirs], gcore, wcore_sems.at[0], sibling)

    def weight_x():
        arrived(gcore, wcore_sems.at[0], sibling)
        gpart[mine, :] = gpart[mine, :] + gcore[...]
        for i in range(1, 4):
            at = pl.ds(k * 64 + ((x + i) % 4) * GROW, GROW)
            sends.start(gpart.at[at], gx4.at[i], wx_sems.at[i], xs[i])

    def weight_y():
        for i in range(1, 4):
            arrived(gx4.at[i], wx_sems.at[i], xs[4 - i])
        gx4[0] = gpart[share, :] + gx4[1] + gx4[2] + gx4[3]
        for i in range(1, 4):
            sends.start(gx4.at[0], gy4.at[i], wy_sems.at[i], ys[i])

    def weight_z():
        for i in range(1, 4):
            arrived(gy4.at[i], wy_sems.at[i], ys[4 - i])
        gy4[0] = gx4[0] + gy4[1] + gy4[2] + gy4[3]
        for i in range(1, 8):
            sends.start(gy4.at[0], gz8.at[i], wz_sems.at[i], zs[i])

    def weight_share():
        for i in range(1, 8):
            arrived(gz8.at[i], wz_sems.at[i], zs[8 - i])
        total = gy4[0]
        for i in range(1, 8):
            total = total + gz8[i]
        final[share, :] = total
        for i in range(1, 4):
            sends.start(final.at[share], final.at[share], wg_sems.at[i], xs[i])

    def weight_core():
        for i in range(1, 4):
            from_x = pl.ds(k * 64 + ((x + 4 - i) % 4) * GROW, GROW)
            arrived(final.at[from_x], wg_sems.at[i], xs[4 - i])
        sends.start(final.at[mine], final.at[mine], wc_sems.at[0], sibling)

    for p in range(4):
        step_a(p)
    steps = {
        "a": step_a, "b": step_b, "c": step_c, "wg": weight_grad, "wx": weight_x, "wy": weight_y,
        "wz": weight_z, "ws": weight_share, "wc": weight_core,
    }
    for name, *which in LAST_ORDER:
        steps[name](*which)
    weight = w_ref[...]
    for p in range(4):
        arrived(zin.at[rows(p)], z_sems.at[p], over)
    for p in (4, 5):
        start = PIECES[p][1]

        def output(at):
            here = pl.ds(start + at.start, at.size)
            value = own[dest(0, p), here, :].astype(F32) + zin[here, :].astype(F32)
            for term in (far(p, 0), far(p, 1)):
                value = value + term[at, :].astype(F32)
            high = value.astype(BF16)
            low = (value - high.astype(F32)).astype(BF16)
            dims = (((1,), (1,)), ((), ()))
            result = lax.dot_general(high, weight, dims, preferred_element_type=F32)
            result = result + lax.dot_general(low, weight, dims, preferred_element_type=F32)
            gx_ref[here, :] = result.astype(BF16)

        each_chunk(PIECES[p][2], 256, output)
    arrived(final.at[theirs], wc_sems.at[0], sibling)
    gw_ref[...] = final[...]
    sends.finish()


def last(back, x, weight):
    vmem, anywhere = (pl.BlockSpec(memory_space=m) for m in (pltpu.VMEM, pl.ANY))
    dma = pltpu.SemaphoreType.DMA
    n = len(PIECES)
    return pl.pallas_call(
        last_kernel,
        out_shape=(jax.ShapeDtypeStruct((ROWS, 128), BF16), jax.ShapeDtypeStruct((128, 128), F32)),
        in_specs=[anywhere, anywhere, vmem],
        out_specs=(vmem, vmem),
        scratch_shapes=[
            pltpu.VMEM((8, ROWS, 128), BF16),
            pltpu.VMEM((8, ROWS, 128), BF16),
            pltpu.VMEM((n, 2, 256, 128), BF16),
            pltpu.VMEM((n, 2, 512, 128), BF16),
            pltpu.VMEM((ROWS, 128), BF16),
            pltpu.VMEM((64, 128), F32),
            pltpu.VMEM((4, GROW, 128), F32),
            pltpu.VMEM((4, GROW, 128), F32),
            pltpu.VMEM((8, GROW, 128), F32),
            pltpu.VMEM((128, 128), F32),
            pltpu.VMEM((128, 128), F32),
            dma((2,)), dma((n, 2)), dma((n, 2)), dma((n,)), dma((48,)),
            dma((1,)), dma((4,)), dma((4,)), dma((8,)), dma((4,)), dma((1,)),
        ],
        compiler_params=pltpu.CompilerParams(
            collective_id=3, has_side_effects=True, vmem_limit_bytes=VMEM_BYTES
        ),
    )(back, x, weight)


def shards(features, weight, tile_values, tile_rows, tile_cols, tile_live, cotangent):
    tiles = tile_values[0, 0]
    rows = tile_rows[0, 0]
    cols = tile_cols[0, 0]
    live = tile_live[0]
    gathered = gather_row(features)
    part = forward(rows, cols, live, gathered.reshape(8 * ROWS, 128), weight, tiles)
    layer_out, grows = middle(part.reshape(32, ROWS, 128), cotangent)
    back = backward(rows, cols, live, grows.reshape(256, 128, 128), tiles)
    grad_x, grad_w = last(back.reshape(8, ROWS, 128), gathered, weight)
    return (layer_out, grad_x, grad_w)


def solution(mesh):
    in_specs = (
        P(("col", "row"), None),
        P(),
        P("row", "col", None, None, None),
        P("row", "col", None),
        P("row", "col", None),
        P("row", "col"),
        P(("row", "col"), None),
    )
    out_specs = (P(("row", "col"), None), P(("col", "row"), None), P())
    return jax.shard_map(shards, mesh=mesh, in_specs=in_specs, out_specs=out_specs, check_vma=False)
```

time: 192 us -> 180 us (0.938)
  Pallas kernels: 187 us -> 175 us
    pallas_call x1, Pallas kernels: 99.4 us -> 87.6 us  [middle(): pl.pallas_call(middle_kernel, out_shape=(jax.ShapeDtypeStruct((ROWS, 128)...]
    pallas_call x1, Pallas kernels: 42.8 us -> 37.1 us  [last(): pl.pallas_call(last_kernel, out_shape=(jax.ShapeDtypeStruct((ROWS, 128),...]
    pallas_call x1, Pallas kernels: 6.49 us -> 8.56 us  [backward(): pl.pallas_call(backward_kernel, out_shape=jax.ShapeDtypeStruct((64, 128,...]
where the time goes in v2:
time: 180 us
  Pallas kernels  175 us (97%)
  local copies, waits for them, and re-layouts  3.85 us (2%)
    pallas_call x1, Pallas kernels, middle(): pl.pallas_call(middle_kernel, out_shape=(jax.ShapeDtypeStruct((ROWS, 128)...  87.6 us
    pallas_call x1, Pallas kernels, last(): pl.pallas_call(last_kernel, out_shape=(jax.ShapeDtypeStruct((ROWS, 128),...  37.1 us
    pallas_call x1, Pallas kernels, gather_row(): pl.pallas_call(gather_row_kernel, out_shape=jax.ShapeDtypeStruct((8, ROWS...  29.9 us
    pallas_call x1, Pallas kernels, forward(): pl.pallas_call(forward_kernel, out_shape=jax.ShapeDtypeStruct((256, 128,...  11.5 us
    pallas_call x1, Pallas kernels, backward(): pl.pallas_call(backward_kernel, out_shape=jax.ShapeDtypeStruct((64, 128,...  8.56 us
    unnamed x5, local copies, waits for them, and re-layouts  3.85 us

profile of v2, /device:TPU:1, one launch (start us, length us, event | category | flops | bytes accessed | tf_op | source)
XLA Modules:
  0.0 179.8 jit_solution(2538238884421856177)
XLA Ops:
  1.3 29.9 %shard_map.94.x_ref = bf16[8,1024,128]{2,1,0:T(8,128)(2,1)} custom-call(bf16[1024,128]{1,0:T(8,128)(2,1)} %x_ref.1), custom_call_target="tpu_custom_call" | custom-call | tf_op jit(solution)/shard_map/pallas_call | solution.py:134
  31.2 11.5 %shard_map.95 = bf16[256,128,128]{2,1,0:T(8,128)(2,1)} custom-call(s32[64]{0:T(128)} %bitcast.16, s32[64]{0:T(128)} %bitcast.18, s32[1]{0:T(128)} %bitcast.8.live_ref, bf16[8192,128]{1,0:T(8,128)(2,1)} %bitcast.11, bf16[128,128]{1,0:T(8,128)(2,1)} %w_ref.3, bf16[64,128,128]{2,1,0:T(8,128)(2,1)} %bitcast.12), custom_call_target="tpu_custom_call" | custom-call | tf_op jit(solution)/shard_map/pallas_call | solution.py:196
  42.7 87.6 %shard_map.96 = (bf16[1024,128]{1,0:T(8,128)(2,1)}, bf16[32,1024,128]{2,1,0:T(8,128)(2,1)}) custom-call(bf16[32,1024,128]{2,1,0:T(8,128)(2,1)} %bitcast.10, bf16[1024,128]{1,0:T(8,128)(2,1)} %cot_ref.1), custom_call_target="tpu_custom_call" | custom-call | tf_op jit(solution)/shard_map/pallas_call | solution.py:359
  130.3 8.6 %shard_map.97 = bf16[64,128,128]{2,1,0:T(8,128)(2,1)} custom-call(s32[64]{0:T(128)} %bitcast.17, s32[64]{0:T(128)} %bitcast.19, s32[1]{0:T(128)} %bitcast.9.live_ref, bf16[256,128,128]{2,1,0:T(8,128)(2,1)} %bitcast.15, bf16[64,128,128]{2,1,0:T(8,128)(2,1)} %bitcast.13), custom_call_target="tpu_custom_call" | custom-call | tf_op jit(solution)/shard_map/pallas_call | solution.py:433
  138.8 0.0 copy-start
  138.8 37.1 %shard_map.98 = (bf16[1024,128]{1,0:T(8,128)(2,1)}, f32[128,128]{1,0:T(8,128)}) custom-call(bf16[8,1024,128]{2,1,0:T(8,128)(2,1)} %bitcast.14, bf16[8,1024,128]{2,1,0:T(8,128)(2,1)} %shard_map.94.x_ref, bf16[128,128]{1,0:T(8,128)(2,1)} %w_ref.3), custom_call_target="tpu_custom_call" | custom-call | tf_op jit(solution)/shard_map/pallas_call | solution.py:606
  176.0 0.0 copy-done
  176.0 0.7 copy.14
  176.7 1.7 copy.15
  178.4 1.5 copy.16
Async XLA Ops:
  138.8 37.2 %copy-start = (bf16[1024,128]{1,0:T(8,128)(2,1)S(1)}, bf16[1024,128]{1,0:T(8,128)(2,1)}, u32[]{:S(2)}) copy-start(bf16[1024,128]{1,0:T(8,128)(2,1)} %get-tuple-element.14) | copy-start | bytes 786436

commit v3 on v2

--- a/solution.py
+++ b/solution.py
@@ -78,7 +78,31 @@
 G1_ORDER = (("far", 0), ("near", 2), ("far", 1), ("near", 3), ("far", 2), ("near", 4), ("far", 3), ("near", 5), ("far", 4), ("far", 5))
 
 
-def gather_row_kernel(x_ref, out_ref, local_sem, send_sems, z_sems, near_sems, far_sems):
+def slot_table(rows, cols, live):
+    slots = rows.shape[1]
+    i = lax.broadcasted_iota(jnp.int32, (slots, slots), 0)
+    lane = lax.broadcasted_iota(jnp.int32, (slots, slots), 1)
+
+    def upright(v):
+        return jnp.sum(jnp.where(i == lane, v, 0.0), axis=1, keepdims=True)
+
+    owner = jnp.floor(rows * 0.125)
+    owner_up, rows_up, cols_up = upright(owner), upright(rows), upright(cols)
+    earlier = jnp.where((owner_up == owner) & (lane < i), 1.0, 0.0)
+    rank = jnp.sum(earlier, axis=1, keepdims=True)
+    slot = lax.broadcasted_iota(jnp.int32, (slots, 128), 0)
+    entry = lax.broadcasted_iota(jnp.int32, (slots, 128), 1).astype(F32)
+    chosen = jnp.where((owner_up * 4.0 + rank == entry) & (slot < live), 1.0, 0.0)
+
+    def pick(v):
+        return jnp.sum(chosen * v, axis=0, keepdims=True)
+
+    return pick(slot.astype(F32) - 64.0) + 64.0, pick(rows_up - owner_up * 8.0), pick(cols_up)
+
+
+def gather_row_kernel(
+    live_ref, x_ref, rows_ref, cols_ref, out_ref, table_ref, local_sem, send_sems, z_sems, near_sems, far_sems
+):
     x, y, zh, zl, k = place()
     right, left = device(x, (y + 1) % 4, zh, zl, k), device(x, (y + 3) % 4, zh, zl, k)
     over = device(x, y, 1 - zh, zl, k)
@@ -120,6 +144,10 @@
         src = piece(y + 1, p, 1)
         sends.start(src, src, far_sems.at[p, 1], left)
 
+    table_ref[...] = jnp.zeros((8, 128), jnp.int32)
+    values = slot_table(rows_ref[...].astype(F32), cols_ref[...].astype(F32), live_ref[0])
+    for n, value in enumerate(values):
+        table_ref[n : n + 1, :] = value.astype(jnp.int32)
     for what, p in G1_ORDER:
         (near if what == "near" else far)(p)
     for p in range(len(G1)):
@@ -129,13 +157,17 @@
     mine.wait()
 
 
-def gather_row(features):
+def gather_row(features, rows, cols, live):
     n = len(G1)
+    smem, vmem, anywhere = (pl.BlockSpec(memory_space=m) for m in (pltpu.SMEM, pltpu.VMEM, pl.ANY))
     return pl.pallas_call(
         gather_row_kernel,
-        out_shape=jax.ShapeDtypeStruct((8, ROWS, 128), BF16),
-        in_specs=[pl.BlockSpec(memory_space=pl.ANY)],
-        out_specs=pl.BlockSpec(memory_space=pl.ANY),
+        out_shape=(
+            jax.ShapeDtypeStruct((8, ROWS, 128), BF16),
+            jax.ShapeDtypeStruct((8, 128), jnp.int32),
+        ),
+        in_specs=[smem, anywhere, vmem, vmem],
+        out_specs=(anywhere, vmem),
         scratch_shapes=[
             pltpu.SemaphoreType.DMA,
             pltpu.SemaphoreType.DMA((len(G1_OVER) + 4 * n,)),
@@ -146,67 +178,7 @@
         compiler_params=pltpu.CompilerParams(
             collective_id=1, has_side_effects=True, vmem_limit_bytes=VMEM_BYTES
         ),
-    )(features)
-
-
-TURN = 4
-
-
-def forward_kernel(rows_ref, cols_ref, live_ref, x_ref, w_ref, tiles_ref, out_ref, xv, proj, tiles, acc, sems):
-    load_x = pltpu.make_async_copy(x_ref, xv, sems.at[0])
-    load_t = pltpu.make_async_copy(tiles_ref, tiles, sems.at[1])
-    load_x.start()
-    load_t.start()
-
-    def clear(i, carry):
-        acc[pl.ds(i * 4, 4)] = jnp.zeros((4, 128, 128), BF16)
-        return carry
-
-    lax.fori_loop(0, 64, clear, 0)
-    load_x.wait()
-    weight = w_ref[...]
-
-    def project(i, carry):
-        block = xv[pl.ds(pl.multiple_of(i * 512, 512), 512), :]
-        value = jnp.dot(block, weight, preferred_element_type=F32).astype(BF16)
-        proj[pl.ds(i * 4, 4)] = value.reshape(4, 128, 128)
-        return carry
-
-    lax.fori_loop(0, 16, project, 0)
-    load_t.wait()
-
-    def turn(i, carry):
-        products = []
-        for u in range(TURN):
-            s = i * TURN + u
-            products.append(jnp.dot(tiles[s], proj[cols_ref[s]], preferred_element_type=F32))
-        for u in range(TURN):
-            b = rows_ref[i * TURN + u]
-            acc[b] = (acc[b].astype(F32) + products[u]).astype(BF16)
-        return carry
-
-    lax.fori_loop(0, live_ref[0] // TURN, turn, 0)
-    store = pltpu.make_async_copy(acc, out_ref, sems.at[2])
-    store.start()
-    store.wait()
-
-
-def forward(rows, cols, live, x, weight, tiles):
-    smem, vmem, anywhere = (pl.BlockSpec(memory_space=m) for m in (pltpu.SMEM, pltpu.VMEM, pl.ANY))
-    return pl.pallas_call(
-        forward_kernel,
-        out_shape=jax.ShapeDtypeStruct((256, 128, 128), BF16),
-        in_specs=[smem, smem, smem, anywhere, vmem, anywhere],
-        out_specs=anywhere,
-        scratch_shapes=[
-            pltpu.VMEM((8 * ROWS, 128), BF16),
-            pltpu.VMEM((64, 128, 128), BF16),
-            pltpu.VMEM((64, 128, 128), BF16),
-            pltpu.VMEM((256, 128, 128), BF16),
-            pltpu.SemaphoreType.DMA((3,)),
-        ],
-        compiler_params=pltpu.CompilerParams(vmem_limit_bytes=VMEM_BYTES),
-    )(rows, cols, live, x, weight, tiles)
+    )(live, features, rows, cols)
 
 
 HALF = ROWS // 2
@@ -215,6 +187,7 @@
     (2, 2), (1, 2), (3, 2), (2, 1), (2, 3), (0, 2), (1, 1), (1, 3),
     (2, 0), (3, 1), (3, 3), (1, 0), (0, 1), (0, 3), (3, 0), (0, 0),
 )
+AHEAD = 2
 MIDDLE_ORDER = (
     ("a", 2, 0), ("a", 1, 0), ("a", 3, 0), ("b", 2, 0), ("a", 0, 0), ("b", 1, 0), ("a", 2, 1), ("b", 3, 0),
     ("c", 2, 0), ("a", 1, 1), ("b", 0, 0), ("c", 1, 0), ("a", 3, 1), ("b", 2, 1), ("c", 3, 0), ("a", 0, 1),
@@ -227,8 +200,8 @@
 
 
 def middle_kernel(
-    part_ref, cot_ref, layer_ref, grows_ref,
-    own, sib, s1, s2, zin, gown,
+    table_ref, x_ref, w_ref, tiles_ref, cot_ref, layer_ref, grows_ref,
+    xv, proj, tiles, products, both, sib, s1, s2, zin, gown,
     load_sems, sib_sems, s1_sems, s2_sems, z_sems, send_sems,
     gz_sems, gnear_sems, gfar_sems, gsib_sems, mine_sems,
 ):
@@ -237,23 +210,54 @@
     sibling = device(x, y, zh, zl, 1 - k)
     along = [None] + [device(x, y, zh, (zl + j) % 4, k) for j in range(1, 4)]
     halves = (pl.ds(0, HALF), pl.ds(HALF, HALF))
-    loads = {}
-    for j, m in NEEDED:
-        c = ((zl + j) % 4) * 8 + ((x + m) % 4) * 2 + k
-        loads[j, m] = pltpu.make_async_copy(part_ref.at[c], own.at[j, m], load_sems.at[j, m])
-        loads[j, m].start()
+    own = both.at[1]
+    load_x = pltpu.make_async_copy(x_ref, xv, load_sems.at[0])
+    load_x.start()
+    load_t = pltpu.make_async_copy(tiles_ref, tiles.at[pl.ds(0, 64)], load_sems.at[1])
+    load_t.start()
+    tiles[64] = jnp.zeros((128, 128), BF16)
+    load_x.wait()
+
+    def project(i, carry):
+        rows = xv[pl.ds(pl.multiple_of(i * 512, 512), 512), :]
+        value = jnp.dot(rows, w_ref[...], preferred_element_type=F32).astype(BF16)
+        proj[pl.ds(i * 4, 4)] = value.reshape(4, 128, 128)
+        return carry
+
+    lax.fori_loop(0, 16, project, 0)
+    load_t.wait()
     greet([right, left, sibling] + along[1:])
     sends = Sends(send_sems)
-    for q in range(2):
-        for j, m in NEEDED:
-            c = ((zl + j) % 4) * 8 + ((x + m) % 4) * 2 + (1 - k)
-            sends.start(part_ref.at[c, halves[q]], sib.at[j, m, halves[q]], sib_sems.at[j, m, q], sibling)
-    loaded = set()
+
+    def produce(j, m):
+        def side(i, carry):
+            core = (1 - k) + i * (2 * k - 1)
+            entry = (((zl + j) % 4) * 8 + ((x + m) % 4) * 2 + core) * 4
+            for n in range(4):
+                products[n] = jnp.dot(
+                    tiles[table_ref[0, entry + n]], proj[table_ref[2, entry + n]], preferred_element_type=F32
+                )
+
+            def place_block(b, inner):
+                total = jnp.zeros((128, 128), F32)
+                for n in range(4):
+                    total = total + jnp.where(table_ref[1, entry + n] == b, products[n], 0.0)
+                both[i, j, m, pl.ds(pl.multiple_of(b * 128, 128), 128), :] = total.astype(BF16)
+                return inner
+
+            lax.fori_loop(0, 8, place_block, 0)
+            return carry
+
+        lax.fori_loop(0, 2, side, 0)
+        for q in range(2):
+            sends.start(both.at[0, j, m, halves[q]], sib.at[j, m, halves[q]], sib_sems.at[j, m, q], sibling)
+
+    produced = []
 
     def joined(j, m, q):
-        if (j, m) not in loaded:
-            loads[j, m].wait()
-            loaded.add((j, m))
+        while len(produced) < len(NEEDED) and len(produced) <= NEEDED.index((j, m)) + AHEAD:
+            produce(*NEEDED[len(produced)])
+            produced.append(True)
         arrived(sib.at[j, m, halves[q]], sib_sems.at[j, m, q], sibling)
 
     def quarters(q):
@@ -353,8 +357,8 @@
         copy.wait()
 
 
-def middle(part, cotangent):
-    vmem, anywhere = (pl.BlockSpec(memory_space=m) for m in (pltpu.VMEM, pl.ANY))
+def middle(table, x, weight, tiles, cotangent):
+    smem, vmem, anywhere = (pl.BlockSpec(memory_space=m) for m in (pltpu.SMEM, pltpu.VMEM, pl.ANY))
     dma = pltpu.SemaphoreType.DMA
     return pl.pallas_call(
         middle_kernel,
@@ -362,22 +366,29 @@
             jax.ShapeDtypeStruct((ROWS, 128), BF16),
             jax.ShapeDtypeStruct((32, ROWS, 128), BF16),
         ),
-        in_specs=[anywhere, vmem],
+        in_specs=[smem, anywhere, vmem, anywhere, vmem],
         out_specs=(vmem, anywhere),
         scratch_shapes=[
-            pltpu.VMEM((4, 4, ROWS, 128), BF16),
+            pltpu.VMEM((8 * ROWS, 128), BF16),
+            pltpu.VMEM((64, 128, 128), BF16),
+            pltpu.VMEM((65, 128, 128), BF16),
+            pltpu.VMEM((4, 128, 128), F32),
+            pltpu.VMEM((2, 4, 4, ROWS, 128), BF16),
             pltpu.VMEM((4, 4, ROWS, 128), BF16),
             pltpu.VMEM((2, 4, 2, QUARTER, 128), BF16),
             pltpu.VMEM((2, 4, 2, HALF, 128), BF16),
             pltpu.VMEM((2, 3, HALF, 128), BF16),
             pltpu.VMEM((ROWS, 128), BF16),
-            dma((4, 4)), dma((4, 4, 2)), dma((2, 4, 2)), dma((2, 4, 2)), dma((2, 3)), dma((160,)),
+            dma((2,)), dma((4, 4, 2)), dma((2, 4, 2)), dma((2, 4, 2)), dma((2, 3)), dma((160,)),
             dma((2, 3)), dma((2, 4, 2)), dma((2, 4, 2)), dma((2, 4, 5)), dma((2,)),
         ],
         compiler_params=pltpu.CompilerParams(
             collective_id=2, has_side_effects=True, vmem_limit_bytes=VMEM_BYTES
         ),
-    )(part, cotangent)
+    )(table, x, weight, tiles, cotangent)
+
+
+TURN = 4
 
 
 def backward_kernel(rows_ref, cols_ref, live_ref, g_ref, tiles_ref, out_ref, gv, tiles, acc, outv, sems, g_sems):
@@ -634,9 +645,8 @@
     rows = tile_rows[0, 0]
     cols = tile_cols[0, 0]
     live = tile_live[0]
-    gathered = gather_row(features)
-    part = forward(rows, cols, live, gathered.reshape(8 * ROWS, 128), weight, tiles)
-    layer_out, grows = middle(part.reshape(32, ROWS, 128), cotangent)
+    gathered, table = gather_row(features, tile_rows[0], tile_cols[0], live)
+    layer_out, grows = middle(table, gathered.reshape(8 * ROWS, 128), weight, tiles, cotangent)
     back = backward(rows, cols, live, grows.reshape(256, 128, 128), tiles)
     grad_x, grad_w = last(back.reshape(8, ROWS, 128), gathered, weight)
     return (layer_out, grad_x, grad_w)

time: 180 us -> 176 us (0.978)
  Pallas kernels: 175 us -> 170 us
    pallas_call x2 -> x1, Pallas kernels: 41.4 us -> 31.1 us  [gather_row(): pl.pallas_call(gather_row_kernel, out_shape=(jax.ShapeDtypeStruct((8, ROW...]
    pallas_call x1, Pallas kernels: 37.1 us -> 41.9 us  [last(): pl.pallas_call(last_kernel, out_shape=(jax.ShapeDtypeStruct((ROWS, 128),...]
    pallas_call x1, Pallas kernels: 87.6 us -> 92.1 us  [middle(): pl.pallas_call(middle_kernel, out_shape=(jax.ShapeDtypeStruct((ROWS, 128)...]
    pallas_call x1, Pallas kernels: 8.56 us -> 4.97 us  [backward(): pl.pallas_call(backward_kernel, out_shape=jax.ShapeDtypeStruct((64, 128,...]
where the time goes in v3:
time: 176 us; the launch traced here: 175 us
  Pallas kernels  170 us (97%)
  local copies, waits for them, and re-layouts  3.85 us (2%)
    pallas_call x1, Pallas kernels, middle(): pl.pallas_call(middle_kernel, out_shape=(jax.ShapeDtypeStruct((ROWS, 128)...  92.1 us
    pallas_call x1, Pallas kernels, last(): pl.pallas_call(last_kernel, out_shape=(jax.ShapeDtypeStruct((ROWS, 128),...  41.9 us
    pallas_call x1, Pallas kernels, gather_row(): pl.pallas_call(gather_row_kernel, out_shape=(jax.ShapeDtypeStruct((8, ROW...  31.1 us
    pallas_call x1, Pallas kernels, backward(): pl.pallas_call(backward_kernel, out_shape=jax.ShapeDtypeStruct((64, 128,...  4.97 us
    unnamed x5, local copies, waits for them, and re-layouts  3.85 us

profile of v3, /device:TPU:1, one launch (start us, length us, event | category | flops | bytes accessed | tf_op | source)
XLA Modules:
  0.0 175.3 jit_solution(10769686529335241389)
XLA Ops:
  1.3 31.1 %shard_map.94 = (bf16[8,1024,128]{2,1,0:T(8,128)(2,1)}, s32[8,128]{1,0:T(8,128)}) custom-call(s32[1]{0:T(128)} %bitcast.9.live_ref, bf16[1024,128]{1,0:T(8,128)(2,1)} %x_ref.1, s32[1,64]{1,0:T(1,128)} %bitcast.16, s32[1,64]{1,0:T(1,128)} %bitcast.18), custom_call_target="tpu_custom_call" | custom-call | tf_op jit(solution)/shard_map/pallas_call | solution.py:163
  32.4 92.1 %shard_map.95 = (bf16[1024,128]{1,0:T(8,128)(2,1)}, bf16[32,1024,128]{2,1,0:T(8,128)(2,1)}) custom-call(s32[8,128]{1,0:T(8,128)} %get-tuple-element.9.table_ref, bf16[8192,128]{1,0:T(8,128)(2,1)} %bitcast.15, bf16[128,128]{1,0:T(8,128)(2,1)} %w_ref.3, bf16[64,128,128]{2,1,0:T(8,128)(2,1)} %bitcast.11, bf16[1024,128]{1,0:T(8,128)(2,1)} %cot_ref.1), custom_call_target="tpu_custom_call" | custom-call | tf_op jit(solution)/shard_map/pallas_call | solution.py:363
  124.5 5.0 %shard_map.96 = bf16[64,128,128]{2,1,0:T(8,128)(2,1)} custom-call(s32[64]{0:T(128)} %bitcast.17, s32[64]{0:T(128)} %bitcast.19, s32[1]{0:T(128)} %bitcast.10.live_ref, bf16[256,128,128]{2,1,0:T(8,128)(2,1)} %bitcast.14, bf16[64,128,128]{2,1,0:T(8,128)(2,1)} %bitcast.12), custom_call_target="tpu_custom_call" | custom-call | tf_op jit(solution)/shard_map/pallas_call | solution.py:444
  129.4 0.0 copy-start
  129.5 41.9 %shard_map.97 = (bf16[1024,128]{1,0:T(8,128)(2,1)}, f32[128,128]{1,0:T(8,128)}) custom-call(bf16[8,1024,128]{2,1,0:T(8,128)(2,1)} %bitcast.13, bf16[8,1024,128]{2,1,0:T(8,128)(2,1)} %get-tuple-element.10.x_ref, bf16[128,128]{1,0:T(8,128)(2,1)} %w_ref.3), custom_call_target="tpu_custom_call" | custom-call | tf_op jit(solution)/shard_map/pallas_call | solution.py:617
  171.4 0.0 copy-done
  171.4 0.7 copy.14
  172.1 1.7 copy.15
  173.8 1.5 copy.16
Async XLA Ops:
  129.4 42.0 %copy-start = (bf16[1024,128]{1,0:T(8,128)(2,1)S(1)}, bf16[1024,128]{1,0:T(8,128)(2,1)}, u32[]{:S(2)}) copy-start(bf16[1024,128]{1,0:T(8,128)(2,1)} %get-tuple-element.18) | copy-start | bytes 786436

commit v4 on v0

v4 whole, which is shorter than its diff:
```python
import functools

import jax
import jax.numpy as jnp
from jax import lax
from jax.experimental import pallas as pl
from jax.experimental.pallas import tpu as pltpu
from jax.sharding import PartitionSpec as P

MESH = pl.DeviceIdType.MESH
F32 = jnp.float32
BF16 = jnp.bfloat16
ROWS = 1024
VMEM_BYTES = 56 << 20


def place():
    r, c = lax.axis_index("row"), lax.axis_index("col")
    return (c // 2) % 4, r // 2, r % 2, c // 8, c % 2


def device(x, y, zh, zl, k):
    return (y * 2 + zh, zl * 8 + x * 2 + k)


def remote(src, dst, send, recv, target):
    return pltpu.make_async_remote_copy(
        src_ref=src, dst_ref=dst, send_sem=send, recv_sem=recv, device_id=target, device_id_type=MESH
    )


def greet(partners):
    barrier = pltpu.get_barrier_semaphore()
    for partner in partners:
        pl.semaphore_signal(barrier, inc=1, device_id=partner, device_id_type=MESH)
    pl.semaphore_wait(barrier, len(partners))


class Sends:
    def __init__(self, send_sems):
        self.sems = send_sems
        self.started = []

    def start(self, src, dst, recv, target):
        copy = remote(src, dst, self.sems.at[len(self.started)], recv, target)
        copy.start()
        self.started.append(copy)

    def finish(self):
        for copy in self.started:
            copy.wait_send()


def arrived(ref, recv, me):
    remote(ref, ref, recv, recv, me).wait_recv()


def each_chunk(rows, step, body):
    def go(i, carry):
        body(pl.ds(pl.multiple_of(i * step, step), step))
        return carry

    lax.fori_loop(0, rows // step, go, 0)


def add_into(out, terms, rows, step=128):
    def body(at):
        total = out[at, :].astype(F32)
        for term in terms:
            total = total + term[at, :].astype(F32)
        out[at, :] = total.astype(out.dtype)

    each_chunk(rows, step, body)


G1 = ((0, 0, 512), (0, 512, 512), (1, 0, 256), (1, 256, 256), (1, 512, 256), (1, 768, 256))
G1_OVER = (2, 3, 4, 5)
G1_ORDER = (("far", 0), ("near", 2), ("far", 1), ("near", 3), ("far", 2), ("near", 4), ("far", 3), ("near", 5), ("far", 4), ("far", 5))


def slot_table(rows, cols, live):
    slots = rows.shape[1]
    i = lax.broadcasted_iota(jnp.int32, (slots, slots), 0)
    lane = lax.broadcasted_iota(jnp.int32, (slots, slots), 1)
    alive = lane < live

    def upright(v):
        return jnp.sum(jnp.where(i == lane, v, 0.0), axis=1, keepdims=True)

    def number(condition, axis=1):
        return jnp.sum(jnp.where(condition, 1.0, 0.0), axis=axis, keepdims=True)

    owner = jnp.floor(rows * 0.125)
    owner_up, rows_up, cols_up = upright(owner), upright(rows), upright(cols)
    rank = number(alive & (owner == owner_up) & ((rows < rows_up) | ((rows == rows_up) & (lane < i))))
    same_row = number(alive & (rows == rows_up) & (lane < i))
    position = number(alive & ((cols < cols_up) | ((cols == cols_up) & (lane < i))))
    same_col = number(alive & (cols == cols_up) & (lane < i))
    slot = lax.broadcasted_iota(jnp.int32, (slots, 128), 0)
    entry = lax.broadcasted_iota(jnp.int32, (slots, 128), 1).astype(F32)
    chosen = jnp.where((owner_up * 4.0 + rank == entry) & (slot < live), 1.0, 0.0)
    placed = jnp.where((position == entry) & (slot < live), 1.0, 0.0)

    def pick(mask, v):
        return jnp.sum(mask * v, axis=0, keepdims=True)

    def last_of(base):
        block = entry + base
        count = number((rows_up == block) & (slot < live), 0)
        upto = number((owner_up == jnp.floor(block * 0.125)) & (rows_up <= block) & (slot < live), 0)
        return jnp.where(count > 0.0, upto - 1.0, 4.0)

    count = number((cols_up == entry) & (slot < live), 0)
    upto = number((cols_up <= entry) & (slot < live), 0)
    return (
        pick(chosen, slot.astype(F32) - 64.0) + 64.0,
        pick(chosen, rows_up - owner_up * 8.0),
        pick(chosen, cols_up),
        pick(placed, owner_up * 4.0 + rank),
        pick(placed, jnp.where(same_col > 0.0, 1.0, 0.0)),
        jnp.where(count > 0.0, upto - 1.0, 64.0),
        pick(chosen, jnp.where(same_row > 0.0, 1.0, 0.0)),
        last_of(0.0),
        last_of(128.0),
    )


def gather_row_kernel(
    live_ref, x_ref, rows_ref, cols_ref, out_ref, table_ref, local_sem, send_sems, z_sems, near_sems, far_sems
):
    x, y, zh, zl, k = place()
    right, left = device(x, (y + 1) % 4, zh, zl, k), device(x, (y + 3) % 4, zh, zl, k)
    over = device(x, y, 1 - zh, zl, k)
    greet([right, left, over])
    sends = Sends(send_sems)
    own = y * 2 + zh

    def piece(yy, p, part=None):
        side, start, size = G1[p]
        block = (yy % 4) * 2 + (1 - zh if side else zh)
        if part is not None:
            size = size // 2
            start = start + part * size
        return out_ref.at[block, pl.ds(start, size)]

    mine = pltpu.make_async_copy(x_ref, out_ref.at[own], local_sem)
    for p in G1_OVER:
        _, start, size = G1[p]
        rows = pl.ds(start, size)
        sends.start(x_ref.at[rows], out_ref.at[own, rows], z_sems.at[p], over)
    for p in (0, 1):
        _, start, size = G1[p]
        src = x_ref.at[pl.ds(start, size)]
        sends.start(src, piece(y, p), near_sems.at[p, 0], right)
        sends.start(src, piece(y, p), near_sems.at[p, 1], left)
    mine.start()

    def near(p):
        here = piece(y, p)
        arrived(here, z_sems.at[p], over)
        sends.start(here, here, near_sems.at[p, 0], right)
        sends.start(here, here, near_sems.at[p, 1], left)

    def far(p):
        arrived(piece(y + 3, p), near_sems.at[p, 0], left)
        src = piece(y + 3, p, 0)
        sends.start(src, src, far_sems.at[p, 0], right)
        arrived(piece(y + 1, p), near_sems.at[p, 1], right)
        src = piece(y + 1, p, 1)
        sends.start(src, src, far_sems.at[p, 1], left)

    table_ref[...] = jnp.zeros((16, 128), jnp.int32)
    values = slot_table(rows_ref[...].astype(F32), cols_ref[...].astype(F32), live_ref[0])
    for n, value in enumerate(values):
        table_ref[n : n + 1, :] = value.astype(jnp.int32)
    for what, p in G1_ORDER:
        (near if what == "near" else far)(p)
    for p in range(len(G1)):
        arrived(piece(y + 2, p, 0), far_sems.at[p, 0], left)
        arrived(piece(y + 2, p, 1), far_sems.at[p, 1], right)
    sends.finish()
    mine.wait()


def gather_row(features, rows, cols, live):
    n = len(G1)
    smem, vmem, anywhere = (pl.BlockSpec(memory_space=m) for m in (pltpu.SMEM, pltpu.VMEM, pl.ANY))
    return pl.pallas_call(
        gather_row_kernel,
        out_shape=(
            jax.ShapeDtypeStruct((8, ROWS, 128), BF16),
            jax.ShapeDtypeStruct((16, 128), jnp.int32),
        ),
        in_specs=[smem, anywhere, vmem, vmem],
        out_specs=(anywhere, vmem),
        scratch_shapes=[
            pltpu.SemaphoreType.DMA,
            pltpu.SemaphoreType.DMA((len(G1_OVER) + 4 * n,)),
            pltpu.SemaphoreType.DMA((n,)),
            pltpu.SemaphoreType.DMA((n, 2)),
            pltpu.SemaphoreType.DMA((n, 2)),
        ],
        compiler_params=pltpu.CompilerParams(
            collective_id=1, has_side_effects=True, vmem_limit_bytes=VMEM_BYTES
        ),
    )(live, features, rows, cols)


HALF = ROWS // 2
QUARTER = ROWS // 4
NEEDED = (
    (2, 2), (1, 2), (3, 2), (2, 1), (2, 3), (0, 2), (1, 1), (1, 3),
    (2, 0), (3, 1), (3, 3), (1, 0), (0, 1), (0, 3), (3, 0), (0, 0),
)
AHEAD = 2
PIECES = ((0, 0, 2), (0, 2, 2), (0, 4, 2), (0, 6, 2), (1, 0, 4), (1, 4, 4))
GROW = 16
ORDER = (
    ("a", 0, 2), ("a", 0, 1), ("a", 0, 3), ("b", 0, 2), ("a", 0, 0), ("b", 0, 1), ("a", 1, 2), ("b", 0, 3), ("turn", 0),
    ("c", 0, 2), ("a", 1, 1), ("b", 0, 0), ("c", 0, 1), ("turn", 1), ("a", 1, 3), ("b", 1, 2), ("c", 0, 3), ("turn", 2), ("a", 1, 0),
    ("b", 1, 1), ("c", 0, 0), ("end", 0), ("turn", 3), ("b", 1, 3), ("c", 1, 2), ("turn", 4), ("b", 1, 0), ("near", 0, 0),
    ("c", 1, 1), ("turn", 5), ("near", 0, 1), ("c", 1, 3), ("turn", 6), ("near", 0, 3), ("c", 1, 0), ("end", 1),
    ("far", 0, 0), ("near", 0, 2), ("far", 0, 1), ("near", 1, 0), ("mult", 0, 0, 0), ("turn", 7), ("mult", 0, 1, 0),
    ("far", 0, 3), ("mult", 0, 3, 0), ("near", 1, 1), ("share", 0, 0), ("mult", 0, 0, 3), ("mult", 0, 0, 1),
    ("far", 0, 2), ("near", 1, 3), ("share", 0, 1), ("mult", 0, 1, 3), ("mult", 0, 1, 1), ("mult", 0, 2, 0),
    ("far", 1, 0), ("near", 1, 2), ("share", 0, 3), ("mult", 0, 3, 3), ("mult", 0, 3, 1), ("mult", 0, 0, 2),
    ("far", 1, 1), ("share", 0, 2), ("mult", 0, 2, 3), ("mult", 0, 2, 1), ("mult", 0, 1, 2), ("mult", 0, 3, 2),
    ("mult", 0, 2, 2), ("sum", 0), ("ra", 0, 0), ("ra", 0, 1), ("ra", 0, 2), ("ra", 0, 3),
    ("far", 1, 3), ("share", 1, 0), ("wg", 0), ("mult", 1, 0, 0), ("mult", 1, 1, 0), ("rb", 0, 0), ("rb", 0, 1),
    ("far", 1, 2), ("mult", 1, 3, 0), ("mult", 1, 0, 3), ("rb", 0, 2), ("rb", 0, 3), ("ra", 0, 4), ("ra", 0, 5),
    ("share", 1, 1), ("mult", 1, 0, 1), ("mult", 1, 1, 3), ("mult", 1, 1, 1), ("rc", 0, 0), ("rc", 0, 1),
    ("mult", 1, 2, 0), ("mult", 1, 3, 3), ("mult", 1, 3, 1), ("rc", 0, 2), ("rc", 0, 3),
    ("share", 1, 3), ("mult", 1, 0, 2), ("mult", 1, 1, 2), ("rb", 0, 4), ("rb", 0, 5),
    ("mult", 1, 2, 3), ("mult", 1, 2, 1), ("mult", 1, 3, 2), ("share", 1, 2), ("mult", 1, 2, 2),
    ("sum", 1), ("ra", 1, 0), ("ra", 1, 1), ("ra", 1, 2), ("ra", 1, 3), ("wg", 1), ("wx",),
    ("rb", 1, 0), ("rb", 1, 1), ("rb", 1, 2), ("rb", 1, 3), ("rc", 1, 0), ("wy",), ("rc", 1, 1), ("ra", 1, 4),
    ("ra", 1, 5), ("rc", 1, 2), ("rc", 1, 3), ("wz",), ("rc", 0, 4), ("rc", 0, 5), ("fin", 0), ("layer",),
    ("rb", 1, 4), ("rb", 1, 5), ("ws",), ("rc", 1, 4), ("rc", 1, 5),
)


def swap(value):
    return pltpu.roll(value, 64, 1)


def lower(rows):
    return lax.broadcasted_iota(jnp.int32, (rows, 128), 1) < 64


def pack(value):
    top, bottom = value[:64], value[64:]
    low = lower(64)
    return jnp.where(low, top, swap(bottom)), jnp.where(low, swap(top), bottom)


def unpack(first, second):
    low = lower(64)
    return jnp.concatenate([jnp.where(low, first, swap(second)), jnp.where(low, swap(first), second)], axis=0)


def add_blocks(out, terms, blocks):
    def go(b, carry):
        total = out[b].astype(F32)
        for term in terms:
            total = total + term[b].astype(F32)
        out[b] = total.astype(out.dtype)
        return carry

    lax.fori_loop(0, blocks, go, 0)


def main_kernel(
    table_ref, x_ref, w_ref, tiles_ref, cot_ref, layer_ref, gx_ref, gw_ref,
    xv, proj, tiles, runs, both, sib, s1, s2, zin, cotp, layerp, grows, stage, prods, run, back, t1, t2, tz, gpp,
    xt, gacc, g8, gy4, gz8, gpart, final,
    load_sems, sib_sems, s1_sems, s2_sems, z_sems, send_sems, gz_sems, gnear_sems, gfar_sems, gsib_sems,
    t1_sems, t2_sems, tz_sems, wx_sems, wy_sems, wz_sems, wg_sems,
):
    x, y, zh, zl, k = place()
    z = zh * 4 + zl
    sibling = device(x, y, zh, zl, 1 - k)
    xs = [None] + [device((x + i) % 4, y, zh, zl, k) for i in range(1, 4)]
    ys = [None] + [device(x, (y + i) % 4, zh, zl, k) for i in range(1, 4)]
    zs = [None] + [device(x, y, ((z + i) % 8) // 4, ((z + i) % 8) % 4, k) for i in range(1, 8)]
    along = [None] + [device(x, y, zh, (zl + j) % 4, k) for j in range(1, 4)]
    over = device(x, y, 1 - zh, zl, k)
    right, left, above, below = xs[1], xs[3], ys[1], ys[3]
    first, second = pl.ds(0, QUARTER), pl.ds(QUARTER, QUARTER)

    load_x = pltpu.make_async_copy(x_ref, xv, load_sems.at[0])
    load_x.start()
    load_t = pltpu.make_async_copy(tiles_ref, tiles.at[pl.ds(0, 64)], load_sems.at[1])
    load_t.start()
    tiles[64] = jnp.zeros((128, 128), BF16)
    run[64] = jnp.zeros((64, 128), F32)
    for i in range(2):
        runs[i, 4] = jnp.zeros((2, 64, 128), BF16)
    straight = w_ref[...].astype(F32)
    twice = jnp.concatenate([straight, swap(straight)], axis=1).astype(BF16)
    load_x.wait()

    def project(i, carry):
        rows = xv[pl.ds(i * 4, 4)].reshape(512, 128)
        value = jnp.dot(rows, twice, preferred_element_type=F32).astype(BF16)
        proj[pl.ds(i * 4, 4)] = value.reshape(4, 128, 256)
        return carry

    lax.fori_loop(0, 16, project, 0)
    load_t.wait()
    greet([device((x + i % 4) % 4, y, zh, zl, (k + i // 4) % 2) for i in range(1, 8)] + ys[1:] + zs[1:])
    sends = Sends(send_sems)

    def produce(j, m):
        def side(i, carry):
            core = (1 - k) + i * (2 * k - 1)
            c = ((zl + j) % 4) * 8 + ((x + m) % 4) * 2 + core
            low = lower(64)
            before = None
            for n in range(4):
                entry = c * 4 + n
                value = jnp.dot(tiles[table_ref[0, entry]], proj[table_ref[2, entry]], preferred_element_type=F32)
                value = (
                    jnp.where(low, value[:64, :128], value[64:, 128:]),
                    jnp.where(low, value[:64, 128:], value[64:, :128]),
                )
                if n:
                    same = table_ref[6, entry] == 1
                    value = tuple(v + jnp.where(same, u, 0.0) for v, u in zip(value, before))
                for q in range(2):
                    runs[i, n, q] = value[q].astype(BF16)
                before = value
            for b in range(8):
                at = table_ref[7 + c // 16, (c % 16) * 8 + b]
                for q in range(2):
                    both[i, q, j, m, pl.ds(b * 64, 64), :] = runs[i, at, q]
            return carry

        lax.fori_loop(0, 2, side, 0)
        for q in range(2):
            sends.start(both.at[0, q, j, m], sib.at[q, j, m], sib_sems.at[j, m, q], sibling)

    produced = []

    def joined(j, m, q):
        while len(produced) < len(NEEDED) and len(produced) <= NEEDED.index((j, m)) + AHEAD:
            produce(*NEEDED[len(produced)])
            produced.append(True)
        arrived(sib.at[q, j, m], sib_sems.at[j, m, q], sibling)

    def step_a(q, j):
        joined(j, 2, q)
        add_into(both.at[1, q, j, 2], [sib.at[q, j, 2]], HALF)
        sends.start(both.at[1, q, j, 2, first], s1.at[q, j, 0], s1_sems.at[q, j, 0], right)
        sends.start(both.at[1, q, j, 2, second], s1.at[q, j, 1], s1_sems.at[q, j, 1], left)

    def step_b(q, j):
        for m, side, near, far, target, source in ((1, 0, first, second, right, left), (3, 1, second, first, left, right)):
            joined(j, m, q)
            mine = both.at[1, q, j, m]
            add_into(mine.at[far], [sib.at[q, j, m, far]], QUARTER)
            arrived(s1.at[q, j, side], s1_sems.at[q, j, side], source)
            add_into(mine.at[near], [sib.at[q, j, m, near], s1.at[q, j, side]], QUARTER)
            sends.start(mine, s2.at[q, j, side], s2_sems.at[q, j, side], target)

    def step_c(q, j):
        joined(j, 0, q)
        arrived(s2.at[q, j, 0], s2_sems.at[q, j, 0], left)
        arrived(s2.at[q, j, 1], s2_sems.at[q, j, 1], right)
        if j:
            mine = both.at[1, q, j, 0]
            add_into(mine, [sib.at[q, j, 0], s2.at[q, j, 0], s2.at[q, j, 1]], HALF)
            sends.start(mine, zin.at[q, j - 1], z_sems.at[q, j - 1], along[j])

    def place_of(j, m, core):
        return ((zl + 4 - j) % 4) * 8 + ((x + m) % 4) * 2 + core

    def block(q, j, m, part=None, core=None):
        at = grows.at[q, place_of(j, m, k if core is None else core)]
        return at if part is None else at.at[pl.ds(part * 4, 4)]

    def pack_cotangent():
        def go(b, carry):
            value = cot_ref[pl.ds(pl.multiple_of(b * 128, 128), 128), :].astype(F32)
            for q, part in enumerate(pack(value)):
                cotp[q, pl.ds(pl.multiple_of(b * 64, 64), 64), :] = part
            return carry

        lax.fori_loop(0, 8, go, 0)

    def end(q):
        if q == 0:
            pack_cotangent()
        for j in range(1, 4):
            arrived(zin.at[q, j - 1], z_sems.at[q, j - 1], along[4 - j])
        here = place_of(0, 0, k)

        def finish(b, carry):
            at = pl.ds(pl.multiple_of(b * 64, 64), 64)
            pre = both[1, q, 0, 0, at, :].astype(F32) + sib[q, 0, 0, at, :].astype(F32)
            for term in (s2.at[q, 0, 0], s2.at[q, 0, 1], zin.at[q, 0], zin.at[q, 1], zin.at[q, 2]):
                pre = pre + term[at, :].astype(F32)
            sigma = jax.nn.sigmoid(pre)
            layerp[q, at, :] = pre * sigma
            slope = sigma * (1.0 + pre * (1.0 - sigma))
            grows[q, here, b] = (cotp[q, at, :] * slope).astype(BF16)
            return carry

        lax.fori_loop(0, 8, finish, 0)
        for j in (1, 3, 2):
            sends.start(block(q, 0, 0), block(q, 0, 0), gz_sems.at[q, j - 1], along[j])

    def layer():
        def go(b, carry):
            at = pl.ds(pl.multiple_of(b * 64, 64), 64)
            value = unpack(layerp[0, at, :], layerp[1, at, :])
            layer_ref[pl.ds(pl.multiple_of(b * 128, 128), 128), :] = value.astype(BF16)
            return carry

        lax.fori_loop(0, 8, go, 0)

    def near(q, j):
        src = block(q, j, 0)
        if j:
            arrived(src, gz_sems.at[q, j - 1], along[4 - j])
        sends.start(src, src, gnear_sems.at[q, j, 0], right)
        sends.start(src, src, gnear_sems.at[q, j, 1], left)
        sends.start(src, src, gsib_sems.at[q, j, 0], sibling)

    def far(q, j):
        arrived(block(q, j, 3), gnear_sems.at[q, j, 0], left)
        sends.start(block(q, j, 3, 0), block(q, j, 3, 0), gfar_sems.at[q, j, 0], right)
        arrived(block(q, j, 1), gnear_sems.at[q, j, 1], right)
        sends.start(block(q, j, 1, 1), block(q, j, 1, 1), gfar_sems.at[q, j, 1], left)
        sends.start(block(q, j, 3), block(q, j, 3), gsib_sems.at[q, j, 1], sibling)
        sends.start(block(q, j, 1), block(q, j, 1), gsib_sems.at[q, j, 2], sibling)

    def share(q, j):
        arrived(block(q, j, 2, 0), gfar_sems.at[q, j, 0], left)
        sends.start(block(q, j, 2, 0), block(q, j, 2, 0), gsib_sems.at[q, j, 3], sibling)
        arrived(block(q, j, 2, 1), gfar_sems.at[q, j, 1], right)
        sends.start(block(q, j, 2, 1), block(q, j, 2, 1), gsib_sems.at[q, j, 4], sibling)

    def mult(q, j, m):
        if m == 2:
            arrived(block(q, j, 2, 0, 1 - k), gsib_sems.at[q, j, 3], sibling)
            arrived(block(q, j, 2, 1, 1 - k), gsib_sems.at[q, j, 4], sibling)
        else:
            arrived(block(q, j, m, None, 1 - k), gsib_sems.at[q, j, {0: 0, 3: 1, 1: 2}[m]], sibling)

        def go(i, carry):
            c = place_of(j, m, i)
            stage[...] = grows[q, c]
            for n in range(4):
                entry = c * 4 + n
                part = stage[table_ref[1, entry]].astype(F32)
                other = swap(part)
                part = jnp.concatenate(
                    [jnp.concatenate([part, other], axis=1), jnp.concatenate([other, part], axis=1)], axis=0
                ).astype(BF16)
                value = lax.dot_general(
                    tiles[table_ref[0, entry]], part, (((0,), (0,)), ((), ())), preferred_element_type=F32
                )
                prods[q, entry] = jnp.where(lower(64), value[:64, :128], value[64:, 128:])
            return carry

        lax.fori_loop(0, 2, go, 0)

    def add_up(q):
        run[0] = prods[q, table_ref[3, 0]]

        def go(p, carry):
            run[p] = prods[q, table_ref[3, p]] + jnp.where(table_ref[4, p] == 1, run[p - 1], 0.0)
            return carry

        lax.fori_loop(1, 64, go, 0)

        def place_block(r, carry):
            for b in range(8):
                back[q, r, b] = run[table_ref[5, r * 8 + b]].astype(BF16)
            return carry

        lax.fori_loop(0, 8, place_block, 0)

    def dest(m, p):
        return ((y + m) % 4) * 2 + (zh if PIECES[p][0] else 1 - zh)

    def mine_of(q, m, p, part=None):
        _, start, size = PIECES[p]
        if part is not None:
            size = size // 2
            start = start + part * size
        return back.at[q, dest(m, p), pl.ds(start, size)]

    def t1_of(q, p, side):
        return t1.at[q, p, side, pl.ds(0, PIECES[p][2] // 2)]

    def t2_of(q, p, side):
        return t2.at[q, p, side, pl.ds(0, PIECES[p][2])]

    def row_a(q, p):
        sends.start(mine_of(q, 2, p, 0), t1_of(q, p, 0), t1_sems.at[q, p, 0], above)
        sends.start(mine_of(q, 2, p, 1), t1_of(q, p, 1), t1_sems.at[q, p, 1], below)

    def row_b(q, p):
        for m, side, target, source in ((1, 0, above, below), (3, 1, below, above)):
            arrived(t1_of(q, p, side), t1_sems.at[q, p, side], source)
            add_blocks(mine_of(q, m, p, side), [t1_of(q, p, side)], PIECES[p][2] // 2)
            sends.start(mine_of(q, m, p), t2_of(q, p, side), t2_sems.at[q, p, side], target)

    def row_c(q, p):
        arrived(t2_of(q, p, 0), t2_sems.at[q, p, 0], below)
        arrived(t2_of(q, p, 1), t2_sems.at[q, p, 1], above)
        if PIECES[p][0] == 0:
            add_blocks(mine_of(q, 0, p), [t2_of(q, p, 0), t2_of(q, p, 1)], PIECES[p][2])
            _, start, size = PIECES[p]
            sends.start(mine_of(q, 0, p), tz.at[q, pl.ds(start, size)], tz_sems.at[q, p], over)

    def row_end(q):
        for p in range(4):
            _, start, size = PIECES[p]
            arrived(tz.at[q, pl.ds(start, size)], tz_sems.at[q, p], over)
        for p in (4, 5):
            _, start, size = PIECES[p]

            def go(b, carry):
                value = back[q, dest(0, p), start + b].astype(F32) + tz[q, start + b].astype(F32)
                gpp[q, start + b] = value + t2[q, p, 0, b].astype(F32) + t2[q, p, 1, b].astype(F32)
                return carry

            lax.fori_loop(0, size, go, 0)

    eight = [None] + [device((x + i) % 4, y, zh, zl, (k + i // 4) % 2) for i in range(1, 8)]

    def back_of(i):
        return i // 4 * 4 + (4 - i % 4) % 4

    def part_of(i):
        return pl.ds(((k + i // 4) % 2) * 64 + ((x + i) % 4) * GROW, GROW)

    slice_ = part_of(0)

    def turn(part):
        def go(i, carry):
            b = part * 4 + i
            one = xv[b * 2].astype(F32).T
            two = xv[b * 2 + 1].astype(F32).T
            low = lower(128)
            xt[b, :128] = jnp.where(low, one, swap(two)).astype(BF16)
            xt[b, 128:] = jnp.where(low, swap(one), two).astype(BF16)
            return carry

        lax.fori_loop(0, 4, go, 0)

    def weight_grad(q):
        total = jnp.zeros((256, 128), F32)
        for b in range(32):
            nodes = back[q, b // 4, pl.ds((b % 4) * 2, 2)].reshape(128, 128)
            total = total + jnp.dot(xt[b], nodes, preferred_element_type=F32)
        gacc[q] = jnp.where(lower(128), total[:128] + swap(total[128:]), 0.0)

    def weight_x():
        gpart[...] = gacc[0] + swap(gacc[1])
        for i in range(8):
            if i:
                sends.start(gpart.at[part_of(i)], g8.at[i], wx_sems.at[i], eight[i])

    def weight_y():
        total = gpart[slice_, :]
        for i in range(1, 8):
            arrived(g8.at[i], wx_sems.at[i], eight[back_of(i)])
            total = total + g8[i]
        g8[0] = total
        for i in range(1, 4):
            sends.start(g8.at[0], gy4.at[i], wy_sems.at[i], ys[i])

    def weight_z():
        for i in range(1, 4):
            arrived(gy4.at[i], wy_sems.at[i], ys[4 - i])
        gy4[0] = g8[0] + gy4[1] + gy4[2] + gy4[3]
        for i in range(1, 8):
            sends.start(gy4.at[0], gz8.at[i], wz_sems.at[i], zs[i])

    def weight_share():
        for i in range(1, 8):
            arrived(gz8.at[i], wz_sems.at[i], zs[8 - i])
        total = gy4[0]
        for i in range(1, 8):
            total = total + gz8[i]
        final[slice_, :] = total
        for i in range(1, 8):
            sends.start(final.at[slice_], final.at[slice_], wg_sems.at[i], eight[i])

    steps = {
        "a": step_a, "b": step_b, "c": step_c, "end": end, "near": near, "far": far, "share": share, "mult": mult,
        "sum": add_up, "ra": row_a, "rb": row_b, "rc": row_c, "fin": row_end, "layer": layer,
        "turn": turn, "wg": weight_grad, "wx": weight_x, "wy": weight_y, "wz": weight_z, "ws": weight_share,
    }
    for name, *which in ORDER:
        steps[name](*which)
    row_end(1)
    weight = w_ref[...]

    def output(b, carry):
        value = unpack(gpp[0, b], gpp[1, b])
        high = value.astype(BF16)
        low = (value - high.astype(F32)).astype(BF16)
        dims = (((1,), (1,)), ((), ()))
        result = lax.dot_general(high, weight, dims, preferred_element_type=F32)
        result = result + lax.dot_general(low, weight, dims, preferred_element_type=F32)
        gx_ref[pl.ds(pl.multiple_of(b * 128, 128), 128), :] = result.astype(BF16)
        return carry

    lax.fori_loop(0, 8, output, 0)
    for i in range(1, 8):
        arrived(final.at[part_of(back_of(i))], wg_sems.at[i], eight[back_of(i)])
    gw_ref[...] = final[...]
    sends.finish()


def main(table, x, weight, tiles, cotangent):
    smem, vmem, anywhere = (pl.BlockSpec(memory_space=m) for m in (pltpu.SMEM, pltpu.VMEM, pl.ANY))
    dma = pltpu.SemaphoreType.DMA
    n = len(PIECES)
    return pl.pallas_call(
        main_kernel,
        out_shape=(
            jax.ShapeDtypeStruct((ROWS, 128), BF16),
            jax.ShapeDtypeStruct((ROWS, 128), BF16),
            jax.ShapeDtypeStruct((128, 128), F32),
        ),
        in_specs=[smem, anywhere, vmem, anywhere, vmem],
        out_specs=(vmem, vmem, vmem),
        scratch_shapes=[
            pltpu.VMEM((64, 128, 128), BF16),
            pltpu.VMEM((64, 128, 256), BF16),
            pltpu.VMEM((65, 128, 128), BF16),
            pltpu.VMEM((2, 5, 2, 64, 128), BF16),
            pltpu.VMEM((2, 2, 4, 4, HALF, 128), BF16),
            pltpu.VMEM((2, 4, 4, HALF, 128), BF16),
            pltpu.VMEM((2, 4, 2, QUARTER, 128), BF16),
            pltpu.VMEM((2, 4, 2, HALF, 128), BF16),
            pltpu.VMEM((2, 3, HALF, 128), BF16),
            pltpu.VMEM((2, HALF, 128), F32),
            pltpu.VMEM((2, HALF, 128), F32),
            pltpu.VMEM((2, 32, 8, 64, 128), BF16),
            pltpu.VMEM((8, 64, 128), BF16),
            pltpu.VMEM((2, 128, 64, 128), F32),
            pltpu.VMEM((65, 64, 128), F32),
            pltpu.VMEM((2, 8, 8, 64, 128), BF16),
            pltpu.VMEM((2, n, 2, 2, 64, 128), BF16),
            pltpu.VMEM((2, n, 2, 4, 64, 128), BF16),
            pltpu.VMEM((2, 8, 64, 128), BF16),
            pltpu.VMEM((2, 8, 64, 128), F32),
            pltpu.VMEM((32, 256, 128), BF16),
            pltpu.VMEM((2, 128, 128), F32),
            pltpu.VMEM((8, GROW, 128), F32),
            pltpu.VMEM((4, GROW, 128), F32),
            pltpu.VMEM((8, GROW, 128), F32),
            pltpu.VMEM((128, 128), F32),
            pltpu.VMEM((128, 128), F32),
            dma((2,)), dma((4, 4, 2)), dma((2, 4, 2)), dma((2, 4, 2)), dma((2, 3)), dma((256,)),
            dma((2, 3)), dma((2, 4, 2)), dma((2, 4, 2)), dma((2, 4, 5)),
            dma((2, n, 2)), dma((2, n, 2)), dma((2, n)),
            dma((8,)), dma((4,)), dma((8,)), dma((8,)),
        ],
        compiler_params=pltpu.CompilerParams(
            collective_id=2, has_side_effects=True, vmem_limit_bytes=VMEM_BYTES
        ),
    )(table, x, weight, tiles, cotangent)


def shards(features, weight, tile_values, tile_rows, tile_cols, tile_live, cotangent):
    gathered, table = gather_row(features, tile_rows[0], tile_cols[0], tile_live[0])
    return main(table, gathered.reshape(64, 128, 128), weight, tile_values[0, 0], cotangent)


def solution(mesh):
    in_specs = (
        P(("col", "row"), None),
        P(),
        P("row", "col", None, None, None),
        P("row", "col", None),
        P("row", "col", None),
        P("row", "col"),
        P(("row", "col"), None),
    )
    out_specs = (P(("row", "col"), None), P(("col", "row"), None), P())
    return jax.shard_map(shards, mesh=mesh, in_specs=in_specs, out_specs=out_specs, check_vma=False)
```

time: 727 us -> 166 us (0.23)
  waiting for transfers between devices: 628 us -> 0 us
  Pallas kernels: 0 us -> 159 us
  other arithmetic: 42.8 us -> 0 us
  local copies, waits for them, and re-layouts: 28.7 us -> 4.81 us
  between operations: 13.8 us -> 1.29 us
  matrix products: 12 us -> 0 us
    reduce_scatter x2 -> x0, waiting for transfers between devices: 241 us -> none  [the longest x1 149 us: shards(): lax.psum_scatter(partial_value.reshape(-1, width).astype(jnp.bfloat16), '...]
    psum x1 -> x0, waiting for transfers between devices: 238 us -> none  [shards(): grad_w = lax.psum(weight_term, ('row', 'col'))]
    pallas_call x0 -> x2, Pallas kernels: none -> 159 us  [the longest x1 128 us: main(): pl.pallas_call(main_kernel, out_shape=(jax.ShapeDtypeStruct((ROWS, 128),...]
    all_gather x2 -> x0, waiting for transfers between devices: 149 us -> none  [the longest x1 80.1 us: shards(): projected = lax.all_gather(own_proj, 'row', axis=0, tiled=True)]
    scatter-add x4 -> x0, other arithmetic: 24.8 us -> none  [the longest x2 12.5 us: advance(): return accumulated.at[target_piece].add(product)]
    convert_element_type x3 -> x0, other arithmetic: 15.1 us -> none  [the longest x1 9.19 us: shards(): partial_value.reshape(-1, width).astype(jnp.bfloat16)]
    gather x4 -> x0, local copies, waits for them, and re-layouts: 12.9 us -> none  [the longest x2 8.26 us: advance(): source[row_piece]]
    dot_general x7 -> x0, matrix products: 12 us -> none  [the longest x2 3.31 us: advance(): jnp.einsum('tij,tif->tjf', piece, source[row_piece], preferred_element_ty...]
  transfers between devices with their start and end apart: 5 -> 0, of which waited for: 5 -> 0; matrix products, arithmetic and copies ran while one was open for 1% -> 0% of each run, Pallas kernels for 0% -> 0%
where the time goes in v4:
time: 166 us
  Pallas kernels  159 us (96%)
  local copies, waits for them, and re-layouts  4.81 us (3%)
    pallas_call x1, Pallas kernels, main(): pl.pallas_call(main_kernel, out_shape=(jax.ShapeDtypeStruct((ROWS, 128),...  128 us
    pallas_call x1, Pallas kernels, gather_row(): pl.pallas_call(gather_row_kernel, out_shape=(jax.ShapeDtypeStruct((8, ROW...  31.1 us
    unnamed x3, local copies, waits for them, and re-layouts  4.81 us

profile of v4, /device:TPU:1, one launch (start us, length us, event | category | flops | bytes accessed | tf_op | source)
XLA Modules:
  0.0 165.5 jit_solution(16749844976832230672)
XLA Ops:
  1.3 31.1 %shard_map.94 = (bf16[8,1024,128]{2,1,0:T(8,128)(2,1)}, s32[16,128]{1,0:T(8,128)}) custom-call(s32[1]{0:T(128)} %bitcast.5.live_ref, bf16[1024,128]{1,0:T(8,128)(2,1)} %x_ref.1, s32[1,64]{1,0:T(1,128)} %bitcast.8, s32[1,64]{1,0:T(1,128)} %bitcast.9), custom_call_target="tpu_custom_call" | custom-call | tf_op jit(solution)/shard_map/pallas_call | solution.py:188
  32.4 128.3 %shard_map.95 = (bf16[1024,128]{1,0:T(8,128)(2,1)}, bf16[1024,128]{1,0:T(8,128)(2,1)}, f32[128,128]{1,0:T(8,128)}) custom-call(s32[16,128]{1,0:T(8,128)} %get-tuple-element.5.table_ref, bf16[64,128,128]{2,1,0:T(8,128)(2,1)} %bitcast.7, bf16[128,128]{1,0:T(8,128)(2,1)} %w_ref.1, bf16[64,128,128]{2,1,0:T(8,128)(2,1)} %bitcast.6, bf16[1024,128]{1,0:T(8,128)(2,1)} %cot_ref.1), custom_call_target="tpu_custom_call" | custom-call | tf_op jit(solution)/shard_map/pallas_call | solution.py:624
  160.7 1.7 %copy.14 = bf16[1024,128]{1,0:T(8,128)(2,1)} copy(bf16[1024,128]{1,0:T(8,128)(2,1)} %get-tuple-element.10) | data formatting | bytes 524288
  162.4 1.7 %copy.15 = bf16[1024,128]{1,0:T(8,128)(2,1)} copy(bf16[1024,128]{1,0:T(8,128)(2,1)} %get-tuple-element.11) | data formatting | bytes 524288
  164.1 1.5 copy.16

commit v5 on v4

--- a/solution.py
+++ b/solution.py
@@ -33,7 +33,10 @@
     barrier = pltpu.get_barrier_semaphore()
     for partner in partners:
         pl.semaphore_signal(barrier, inc=1, device_id=partner, device_id_type=MESH)
-    pl.semaphore_wait(barrier, len(partners))
+
+
+def greeted(partners):
+    pl.semaphore_wait(pltpu.get_barrier_semaphore(), len(partners))
 
 
 class Sends:
@@ -71,11 +74,6 @@
         out[at, :] = total.astype(out.dtype)
 
     each_chunk(rows, step, body)
-
-
-G1 = ((0, 0, 512), (0, 512, 512), (1, 0, 256), (1, 256, 256), (1, 512, 256), (1, 768, 256))
-G1_OVER = (2, 3, 4, 5)
-G1_ORDER = (("far", 0), ("near", 2), ("far", 1), ("near", 3), ("far", 2), ("near", 4), ("far", 3), ("near", 5), ("far", 4), ("far", 5))
 
 
 def slot_table(rows, cols, live):
@@ -104,12 +102,14 @@
     def pick(mask, v):
         return jnp.sum(mask * v, axis=0, keepdims=True)
 
-    def last_of(base):
-        block = entry + base
-        count = number((rows_up == block) & (slot < live), 0)
-        upto = number((owner_up == jnp.floor(block * 0.125)) & (rows_up <= block) & (slot < live), 0)
-        return jnp.where(count > 0.0, upto - 1.0, 4.0)
-
+    owners = jnp.where((owner_up == entry) & (slot < live), 1.0, 0.0).astype(BF16)
+    offset = rows_up - owner_up * 8.0
+
+    def per_owner(condition):
+        ones = jnp.where(condition, 1.0, 0.0).astype(BF16)
+        return lax.dot_general(owners, ones, (((0,), (0,)), ((), ())), preferred_element_type=F32)[:32]
+
+    block_count, block_upto = per_owner(offset == entry), per_owner(offset <= entry)
     count = number((cols_up == entry) & (slot < live), 0)
     upto = number((cols_up <= entry) & (slot < live), 0)
     return (
@@ -120,90 +120,25 @@
         pick(placed, jnp.where(same_col > 0.0, 1.0, 0.0)),
         jnp.where(count > 0.0, upto - 1.0, 64.0),
         pick(chosen, jnp.where(same_row > 0.0, 1.0, 0.0)),
-        last_of(0.0),
-        last_of(128.0),
-    )
-
-
-def gather_row_kernel(
-    live_ref, x_ref, rows_ref, cols_ref, out_ref, table_ref, local_sem, send_sems, z_sems, near_sems, far_sems
-):
-    x, y, zh, zl, k = place()
-    right, left = device(x, (y + 1) % 4, zh, zl, k), device(x, (y + 3) % 4, zh, zl, k)
-    over = device(x, y, 1 - zh, zl, k)
-    greet([right, left, over])
-    sends = Sends(send_sems)
-    own = y * 2 + zh
-
-    def piece(yy, p, part=None):
-        side, start, size = G1[p]
-        block = (yy % 4) * 2 + (1 - zh if side else zh)
-        if part is not None:
-            size = size // 2
-            start = start + part * size
-        return out_ref.at[block, pl.ds(start, size)]
-
-    mine = pltpu.make_async_copy(x_ref, out_ref.at[own], local_sem)
-    for p in G1_OVER:
-        _, start, size = G1[p]
-        rows = pl.ds(start, size)
-        sends.start(x_ref.at[rows], out_ref.at[own, rows], z_sems.at[p], over)
-    for p in (0, 1):
-        _, start, size = G1[p]
-        src = x_ref.at[pl.ds(start, size)]
-        sends.start(src, piece(y, p), near_sems.at[p, 0], right)
-        sends.start(src, piece(y, p), near_sems.at[p, 1], left)
-    mine.start()
-
-    def near(p):
-        here = piece(y, p)
-        arrived(here, z_sems.at[p], over)
-        sends.start(here, here, near_sems.at[p, 0], right)
-        sends.start(here, here, near_sems.at[p, 1], left)
-
-    def far(p):
-        arrived(piece(y + 3, p), near_sems.at[p, 0], left)
-        src = piece(y + 3, p, 0)
-        sends.start(src, src, far_sems.at[p, 0], right)
-        arrived(piece(y + 1, p), near_sems.at[p, 1], right)
-        src = piece(y + 1, p, 1)
-        sends.start(src, src, far_sems.at[p, 1], left)
-
-    table_ref[...] = jnp.zeros((16, 128), jnp.int32)
-    values = slot_table(rows_ref[...].astype(F32), cols_ref[...].astype(F32), live_ref[0])
-    for n, value in enumerate(values):
+    ), jnp.where(block_count > 0.0, block_upto - 1.0, 4.0)
+
+
+def table_kernel(live_ref, rows_ref, cols_ref, table_ref):
+    table_ref[...] = jnp.zeros((40, 128), jnp.int32)
+    lists, blocks = slot_table(rows_ref[...].astype(F32), cols_ref[...].astype(F32), live_ref[0])
+    for n, value in enumerate(lists):
         table_ref[n : n + 1, :] = value.astype(jnp.int32)
-    for what, p in G1_ORDER:
-        (near if what == "near" else far)(p)
-    for p in range(len(G1)):
-        arrived(piece(y + 2, p, 0), far_sems.at[p, 0], left)
-        arrived(piece(y + 2, p, 1), far_sems.at[p, 1], right)
-    sends.finish()
-    mine.wait()
-
-
-def gather_row(features, rows, cols, live):
-    n = len(G1)
-    smem, vmem, anywhere = (pl.BlockSpec(memory_space=m) for m in (pltpu.SMEM, pltpu.VMEM, pl.ANY))
+    table_ref[8:40, :] = blocks.astype(jnp.int32)
+
+
+def make_table(live, rows, cols):
+    smem, vmem = (pl.BlockSpec(memory_space=m) for m in (pltpu.SMEM, pltpu.VMEM))
     return pl.pallas_call(
-        gather_row_kernel,
-        out_shape=(
-            jax.ShapeDtypeStruct((8, ROWS, 128), BF16),
-            jax.ShapeDtypeStruct((16, 128), jnp.int32),
-        ),
-        in_specs=[smem, anywhere, vmem, vmem],
-        out_specs=(anywhere, vmem),
-        scratch_shapes=[
-            pltpu.SemaphoreType.DMA,
-            pltpu.SemaphoreType.DMA((len(G1_OVER) + 4 * n,)),
-            pltpu.SemaphoreType.DMA((n,)),
-            pltpu.SemaphoreType.DMA((n, 2)),
-            pltpu.SemaphoreType.DMA((n, 2)),
-        ],
-        compiler_params=pltpu.CompilerParams(
-            collective_id=1, has_side_effects=True, vmem_limit_bytes=VMEM_BYTES
-        ),
-    )(live, features, rows, cols)
+        table_kernel,
+        out_shape=jax.ShapeDtypeStruct((40, 128), jnp.int32),
+        in_specs=[smem, vmem, vmem],
+        out_specs=vmem,
+    )(live, rows, cols)
 
 
 HALF = ROWS // 2
@@ -212,10 +147,13 @@
     (2, 2), (1, 2), (3, 2), (2, 1), (2, 3), (0, 2), (1, 1), (1, 3),
     (2, 0), (3, 1), (3, 3), (1, 0), (0, 1), (0, 3), (3, 0), (0, 0),
 )
-AHEAD = 2
+AHEAD = 1
 PIECES = ((0, 0, 2), (0, 2, 2), (0, 4, 2), (0, 6, 2), (1, 0, 4), (1, 4, 4))
 GROW = 16
+GATHER = ((0, 0, 4), (0, 4, 4), (1, 0, 2), (1, 2, 2), (1, 4, 2), (1, 6, 2))
 ORDER = (
+    ("gz", 2), ("gz", 3), ("gz", 4), ("gz", 5), ("gown",), ("gfar", 0), ("gnear", 2), ("gfar", 1), ("gnear", 3), ("gfar", 2),
+    ("gnear", 4), ("gfar", 3), ("gnear", 5), ("gfar", 4), ("gfar", 5), ("gdone",),
     ("a", 0, 2), ("a", 0, 1), ("a", 0, 3), ("b", 0, 2), ("a", 0, 0), ("b", 0, 1), ("a", 1, 2), ("b", 0, 3), ("turn", 0),
     ("c", 0, 2), ("a", 1, 1), ("b", 0, 0), ("c", 0, 1), ("turn", 1), ("a", 1, 3), ("b", 1, 2), ("c", 0, 3), ("turn", 2), ("a", 1, 0),
     ("b", 1, 1), ("c", 0, 0), ("end", 0), ("turn", 3), ("b", 1, 3), ("c", 1, 2), ("turn", 4), ("b", 1, 0), ("near", 0, 0),
@@ -273,7 +211,7 @@
     table_ref, x_ref, w_ref, tiles_ref, cot_ref, layer_ref, gx_ref, gw_ref,
     xv, proj, tiles, runs, both, sib, s1, s2, zin, cotp, layerp, grows, stage, prods, run, back, t1, t2, tz, gpp,
     xt, gacc, g8, gy4, gz8, gpart, final,
-    load_sems, sib_sems, s1_sems, s2_sems, z_sems, send_sems, gz_sems, gnear_sems, gfar_sems, gsib_sems,
+    load_sems, gz_row, gnear_row, gfar_row, sib_sems, s1_sems, s2_sems, z_sems, send_sems, gz_sems, gnear_sems, gfar_sems, gsib_sems,
     t1_sems, t2_sems, tz_sems, wx_sems, wy_sems, wz_sems, wg_sems,
 ):
     x, y, zh, zl, k = place()
@@ -287,28 +225,76 @@
     right, left, above, below = xs[1], xs[3], ys[1], ys[3]
     first, second = pl.ds(0, QUARTER), pl.ds(QUARTER, QUARTER)
 
-    load_x = pltpu.make_async_copy(x_ref, xv, load_sems.at[0])
+    partners = [device((x + i % 4) % 4, y, zh, zl, (k + i // 4) % 2) for i in range(1, 8)] + ys[1:] + zs[1:]
+    here_row = y * 2 + zh
+    load_x = pltpu.make_async_copy(x_ref, xv.at[here_row], load_sems.at[0])
     load_x.start()
     load_t = pltpu.make_async_copy(tiles_ref, tiles.at[pl.ds(0, 64)], load_sems.at[1])
     load_t.start()
-    tiles[64] = jnp.zeros((128, 128), BF16)
-    run[64] = jnp.zeros((64, 128), F32)
-    for i in range(2):
-        runs[i, 4] = jnp.zeros((2, 64, 128), BF16)
+    greet(partners)
+
     straight = w_ref[...].astype(F32)
     twice = jnp.concatenate([straight, swap(straight)], axis=1).astype(BF16)
-    load_x.wait()
-
-    def project(i, carry):
-        rows = xv[pl.ds(i * 4, 4)].reshape(512, 128)
-        value = jnp.dot(rows, twice, preferred_element_type=F32).astype(BF16)
-        proj[pl.ds(i * 4, 4)] = value.reshape(4, 128, 256)
-        return carry
-
-    lax.fori_loop(0, 16, project, 0)
-    load_t.wait()
-    greet([device((x + i % 4) % 4, y, zh, zl, (k + i // 4) % 2) for i in range(1, 8)] + ys[1:] + zs[1:])
+    greeted(partners)
     sends = Sends(send_sems)
+
+    def gather_at(yy, p, part=None):
+        side, start, size = GATHER[p]
+        row = (yy % 4) * 2 + (1 - zh if side else zh)
+        if part is not None:
+            size = size // 2
+            start = start + part * size
+        return row, start, size
+
+    def gathered(yy, p, part=None):
+        row, start, size = gather_at(yy, p, part)
+        return xv.at[row, pl.ds(start, size)]
+
+    def project(yy, p, part=None):
+        row, start, size = gather_at(yy, p, part)
+        nodes = xv[row, pl.ds(start, size)].reshape(size * 128, 128)
+        value = jnp.dot(nodes, twice, preferred_element_type=F32).astype(BF16)
+        proj[pl.ds(row * 8 + start, size)] = value.reshape(size, 128, 256)
+
+    def gather_z(p):
+        _, start, size = GATHER[p]
+        src = x_ref.at[pl.ds(start, size)]
+        sends.start(src, xv.at[here_row, pl.ds(start, size)], gz_row.at[p], over)
+
+    def gather_own():
+        for p in (0, 1):
+            _, start, size = GATHER[p]
+            src = x_ref.at[pl.ds(start, size)]
+            sends.start(src, gathered(y, p), gnear_row.at[p, 0], above)
+            sends.start(src, gathered(y, p), gnear_row.at[p, 1], below)
+        tiles[64] = jnp.zeros((128, 128), BF16)
+        run[64] = jnp.zeros((64, 128), F32)
+        for i in range(2):
+            runs[i, 4] = jnp.zeros((2, 64, 128), BF16)
+        load_x.wait()
+        for p in (0, 1):
+            project(y, p)
+        load_t.wait()
+
+    def gather_near(p):
+        arrived(gathered(y, p), gz_row.at[p], over)
+        sends.start(gathered(y, p), gathered(y, p), gnear_row.at[p, 0], above)
+        sends.start(gathered(y, p), gathered(y, p), gnear_row.at[p, 1], below)
+        project(y, p)
+
+    def gather_far(p):
+        arrived(gathered(y + 3, p), gnear_row.at[p, 0], below)
+        sends.start(gathered(y + 3, p, 0), gathered(y + 3, p, 0), gfar_row.at[p, 0], above)
+        arrived(gathered(y + 1, p), gnear_row.at[p, 1], above)
+        sends.start(gathered(y + 1, p, 1), gathered(y + 1, p, 1), gfar_row.at[p, 1], below)
+        project(y + 3, p)
+        project(y + 1, p)
+
+    def gather_done():
+        for p in range(len(GATHER)):
+            arrived(gathered(y + 2, p, 0), gfar_row.at[p, 0], below)
+            arrived(gathered(y + 2, p, 1), gfar_row.at[p, 1], above)
+            project(y + 2, p)
 
     def produce(j, m):
         def side(i, carry):
@@ -330,7 +316,7 @@
                     runs[i, n, q] = value[q].astype(BF16)
                 before = value
             for b in range(8):
-                at = table_ref[7 + c // 16, (c % 16) * 8 + b]
+                at = table_ref[8 + c, b]
                 for q in range(2):
                     both[i, q, j, m, pl.ds(b * 64, 64), :] = runs[i, at, q]
             return carry
@@ -542,8 +528,8 @@
     def turn(part):
         def go(i, carry):
             b = part * 4 + i
-            one = xv[b * 2].astype(F32).T
-            two = xv[b * 2 + 1].astype(F32).T
+            one = xv[b // 4, (b % 4) * 2].astype(F32).T
+            two = xv[b // 4, (b % 4) * 2 + 1].astype(F32).T
             low = lower(128)
             xt[b, :128] = jnp.where(low, one, swap(two)).astype(BF16)
             xt[b, 128:] = jnp.where(low, swap(one), two).astype(BF16)
@@ -591,7 +577,8 @@
             sends.start(final.at[slice_], final.at[slice_], wg_sems.at[i], eight[i])
 
     steps = {
-        "a": step_a, "b": step_b, "c": step_c, "end": end, "near": near, "far": far, "share": share, "mult": mult,
+        "gz": gather_z, "gown": gather_own, "gnear": gather_near, "gfar": gather_far,
+        "gdone": gather_done, "a": step_a, "b": step_b, "c": step_c, "end": end, "near": near, "far": far, "share": share, "mult": mult,
         "sum": add_up, "ra": row_a, "rb": row_b, "rc": row_c, "fin": row_end, "layer": layer,
         "turn": turn, "wg": weight_grad, "wx": weight_x, "wy": weight_y, "wz": weight_z, "ws": weight_share,
     }
@@ -631,7 +618,7 @@
         in_specs=[smem, anywhere, vmem, anywhere, vmem],
         out_specs=(vmem, vmem, vmem),
         scratch_shapes=[
-            pltpu.VMEM((64, 128, 128), BF16),
+            pltpu.VMEM((8, 8, 128, 128), BF16),
             pltpu.VMEM((64, 128, 256), BF16),
             pltpu.VMEM((65, 128, 128), BF16),
             pltpu.VMEM((2, 5, 2, 64, 128), BF16),
@@ -658,7 +645,7 @@
             pltpu.VMEM((8, GROW, 128), F32),
             pltpu.VMEM((128, 128), F32),
             pltpu.VMEM((128, 128), F32),
-            dma((2,)), dma((4, 4, 2)), dma((2, 4, 2)), dma((2, 4, 2)), dma((2, 3)), dma((256,)),
+            dma((2,)), dma((6,)), dma((6, 2)), dma((6, 2)), dma((4, 4, 2)), dma((2, 4, 2)), dma((2, 4, 2)), dma((2, 3)), dma((320,)),
             dma((2, 3)), dma((2, 4, 2)), dma((2, 4, 2)), dma((2, 4, 5)),
             dma((2, n, 2)), dma((2, n, 2)), dma((2, n)),
             dma((8,)), dma((4,)), dma((8,)), dma((8,)),
@@ -670,8 +657,8 @@
 
 
 def shards(features, weight, tile_values, tile_rows, tile_cols, tile_live, cotangent):
-    gathered, table = gather_row(features, tile_rows[0], tile_cols[0], tile_live[0])
-    return main(table, gathered.reshape(64, 128, 128), weight, tile_values[0, 0], cotangent)
+    table = make_table(tile_live[0], tile_rows[0], tile_cols[0])
+    return main(table, features.reshape(8, 128, 128), weight, tile_values[0, 0], cotangent)
 
 
 def solution(mesh):

time: 166 us -> 156 us (0.940)
  Pallas kernels: 159 us -> 150 us
    pallas_call x1, Pallas kernels: 31.1 us -> 1.54 us  [make_table(): pl.pallas_call(table_kernel, out_shape=jax.ShapeDtypeStruct((40, 128), jn...]
    pallas_call x1, Pallas kernels: 128 us -> 148 us  [main(): pl.pallas_call(main_kernel, out_shape=(jax.ShapeDtypeStruct((ROWS, 128),...]
where the time goes in v5:
time: 156 us
  Pallas kernels  150 us (96%)
  local copies, waits for them, and re-layouts  4.81 us (3%)
    pallas_call x1, Pallas kernels, main(): pl.pallas_call(main_kernel, out_shape=(jax.ShapeDtypeStruct((ROWS, 128),...  148 us
    unnamed x3, local copies, waits for them, and re-layouts  4.81 us

profile of v5, /device:TPU:1, one launch (start us, length us, event | category | flops | bytes accessed | tf_op | source)
XLA Modules:
  0.0 155.9 jit_solution(2749961729630830784)
XLA Ops:
  1.3 1.5 shard_map.94.table_ref
  2.8 148.3 %shard_map.95 = (bf16[1024,128]{1,0:T(8,128)(2,1)}, bf16[1024,128]{1,0:T(8,128)(2,1)}, f32[128,128]{1,0:T(8,128)}) custom-call(s32[40,128]{1,0:T(8,128)} %shard_map.94.table_ref, bf16[8,128,128]{2,1,0:T(8,128)(2,1)} %bitcast.7, bf16[128,128]{1,0:T(8,128)(2,1)} %w_ref.1, bf16[64,128,128]{2,1,0:T(8,128)(2,1)} %bitcast.6, bf16[1024,128]{1,0:T(8,128)(2,1)} %cot_ref.1), custom_call_target="tpu_custom_call" | custom-call | tf_op jit(solution)/shard_map/pallas_call | solution.py:611
  151.1 1.7 %copy.14 = bf16[1024,128]{1,0:T(8,128)(2,1)} copy(bf16[1024,128]{1,0:T(8,128)(2,1)} %get-tuple-element.6) | data formatting | bytes 524288
  152.8 1.7 %copy.15 = bf16[1024,128]{1,0:T(8,128)(2,1)} copy(bf16[1024,128]{1,0:T(8,128)(2,1)} %get-tuple-element.7) | data formatting | bytes 524288
  154.5 1.5 copy.16

commit v6 on v5

--- a/solution.py
+++ b/solution.py
@@ -656,9 +656,29 @@
     )(table, x, weight, tiles, cotangent)
 
 
+def hand_over_kernel(*refs):
+    sems = refs[6]
+    copies = [pltpu.make_async_copy(refs[i], refs[3 + i], sems.at[i]) for i in range(3)]
+    for copy in copies:
+        copy.start()
+    for copy in copies:
+        copy.wait()
+
+
+def hand_over(*results):
+    anywhere = pl.BlockSpec(memory_space=pl.ANY)
+    return pl.pallas_call(
+        hand_over_kernel,
+        out_shape=tuple(jax.ShapeDtypeStruct(v.shape, v.dtype) for v in results),
+        in_specs=[anywhere] * 3,
+        out_specs=(anywhere,) * 3,
+        scratch_shapes=[pltpu.SemaphoreType.DMA((3,))],
+    )(*results)
+
+
 def shards(features, weight, tile_values, tile_rows, tile_cols, tile_live, cotangent):
     table = make_table(tile_live[0], tile_rows[0], tile_cols[0])
-    return main(table, features.reshape(8, 128, 128), weight, tile_values[0, 0], cotangent)
+    return hand_over(*main(table, features.reshape(8, 128, 128), weight, tile_values[0, 0], cotangent))
 
 
 def solution(mesh):

time: 156 us -> 170 us (1.090)
  Pallas kernels: 150 us -> 169 us
  local copies, waits for them, and re-layouts: 4.81 us -> 0 us
    pallas_call x0 -> x1, Pallas kernels: none -> 19 us  [hand_over(): pl.pallas_call(hand_over_kernel, out_shape=tuple((jax.ShapeDtypeStruct(v....]
    unnamed x3 -> x0, local copies, waits for them, and re-layouts: 4.81 us -> none
where the time goes in v6:
time: 170 us
  Pallas kernels  169 us (99%)
    pallas_call x1, Pallas kernels, main(): pl.pallas_call(main_kernel, out_shape=(jax.ShapeDtypeStruct((ROWS, 128),...  148 us
    pallas_call x1, Pallas kernels, hand_over(): pl.pallas_call(hand_over_kernel, out_shape=tuple((jax.ShapeDtypeStruct(v....  19 us

profile of v6, /device:TPU:1, one launch (start us, length us, event | category | flops | bytes accessed | tf_op | source)
XLA Modules:
  0.0 170.3 jit_solution(4181429244977706923)
XLA Ops:
  1.3 1.5 shard_map.94.table_ref
  2.8 148.3 %shard_map.95 = (bf16[1024,128]{1,0:T(8,128)(2,1)}, bf16[1024,128]{1,0:T(8,128)(2,1)}, f32[128,128]{1,0:T(8,128)}) custom-call(s32[40,128]{1,0:T(8,128)} %shard_map.94.table_ref, bf16[8,128,128]{2,1,0:T(8,128)(2,1)} %bitcast.7, bf16[128,128]{1,0:T(8,128)(2,1)} %w_ref.1, bf16[64,128,128]{2,1,0:T(8,128)(2,1)} %bitcast.6, bf16[1024,128]{1,0:T(8,128)(2,1)} %cot_ref.1), custom_call_target="tpu_custom_call" | custom-call | tf_op jit(solution)/shard_map/pallas_call | solution.py:611
  151.1 19.0 %shard_map.96 = (bf16[1024,128]{1,0:T(8,128)(2,1)}, bf16[1024,128]{1,0:T(8,128)(2,1)}, f32[128,128]{1,0:T(8,128)}) custom-call(bf16[1024,128]{1,0:T(8,128)(2,1)} %get-tuple-element.6.refs_0_, bf16[1024,128]{1,0:T(8,128)(2,1)} %get-tuple-element.7.refs_1_, f32[128,128]{1,0:T(8,128)} %get-tuple-element.8.refs_2_), custom_call_target="tpu_custom_call" | custom-call | tf_op jit(solution)/shard_map/pallas_call | solution.py:670
